TPU v7x, 512 devices: a whole 4x8x8 slice. The times are simulated.
512 devices in a mesh: day: 16 (over z, x_lo), sta: 32 (over y, x_hi, core).
Axes of the slice: x: 4 (x_hi: 2, x_lo: 2; x = x_hi * 2 + x_lo), y: 8, z: 8, core: 2. Of those that a mesh axis runs over, the one named last changes fastest.
Arguments:
- record: bfloat16 [64, 256, 1024], P('day', 'sta'), may hold values from -6 to 6
- alive_mask: int32 [64, 256], replicated, may hold values from 0 to 1
- owners: int32 [4], replicated, may hold values from 0 to 31, as said below
Outputs:
- stacks: float32 [256, 32, 257], P('sta', 'day')
Inputs may be any that keep to these rules, and one draw needn't show every extreme that they name: `owners`: 4 distinct indices of the sta axis, among them always the first and the last.
All inputs are finite; a program needn't handle non-finite values.
Results may differ from a plain program's by a relative error of at most 0.005.
Values may be sent and summed in bfloat16 or wider, within the bound.
No kernel may reach another device: no remote copies, remote signals or barrier semaphores. Data moves between devices by JAX's collectives and lax.ppermute only.
A program may use at most 128 MiB of HBM per device.

v0:
```python
import math

import jax
import jax.numpy as jnp
from jax import lax
from jax.sharding import PartitionSpec as P

MAXLAG = 128
OWNERS = 4


def from_root(block, axis, owner):
    block = jnp.where(lax.axis_index(axis) == owner, block, jnp.zeros_like(block))
    return lax.psum(block, axis)


def forward_table(samples, half_len):
    times = jnp.arange(samples, dtype=jnp.int32)[:, None]
    bins = jnp.arange(1, half_len + 1, dtype=jnp.int32)[None, :]
    phase = (times * bins % samples).astype(jnp.float32) * (2.0 * math.pi / samples)
    return jnp.concatenate(
        [jnp.cos(phase).astype(jnp.bfloat16), (-jnp.sin(phase)).astype(jnp.bfloat16)], axis=1
    )


def lag_table(samples, half_len, reach):
    bins = jnp.arange(1, half_len + 1, dtype=jnp.int32)[:, None]
    shifts = jnp.arange(-reach, reach + 1, dtype=jnp.int32)[None, :]
    phase = (bins * shifts % samples).astype(jnp.float32) * (2.0 * math.pi / samples)
    weight = jnp.where(bins == half_len, 1.0, 2.0).astype(jnp.float32) / math.sqrt(samples)
    return jnp.concatenate([weight * jnp.cos(phase), -weight * jnp.sin(phase)], axis=0).astype(
        jnp.bfloat16
    )


def whiten(record, mask_real, forward):
    windows, stations, samples = record.shape
    half_len = forward.shape[1] // 2
    spectrum = jnp.dot(record.reshape(-1, samples), forward, preferred_element_type=jnp.float32)
    spectrum = spectrum.reshape(windows, stations, 2 * half_len)
    real_part = spectrum[..., :half_len]
    imag_part = spectrum[..., half_len:]
    magnitude = jnp.sqrt(real_part * real_part + imag_part * imag_part)
    level = jnp.mean(magnitude, axis=-1, keepdims=True)
    factor = mask_real[..., None] / (magnitude + 0.3 * level + 1e-06)
    return jnp.concatenate([real_part * factor, imag_part * factor], axis=-1).astype(jnp.bfloat16)


def cross_block(own_block, partner, offset, width):
    half_len = own_block.shape[2] // 2
    own_real = own_block[:, :, offset : offset + width]
    own_imag = own_block[:, :, half_len + offset : half_len + offset + width]
    par_real = partner[:, :, offset : offset + width]
    par_imag = partner[:, :, half_len + offset : half_len + offset + width]
    form = "wmf,wof->mof"
    cross_real = jnp.einsum(
        form, own_real, par_real, preferred_element_type=jnp.float32
    ) + jnp.einsum(form, own_imag, par_imag, preferred_element_type=jnp.float32)
    cross_imag = jnp.einsum(
        form, own_imag, par_real, preferred_element_type=jnp.float32
    ) - jnp.einsum(form, own_real, par_imag, preferred_element_type=jnp.float32)
    return jnp.concatenate([cross_real, cross_imag], axis=-1).astype(jnp.bfloat16)


def cross_lags(own_block, partner, lag_rows):
    half_len = own_block.shape[2] // 2
    width = min(half_len, 256)
    running = jnp.zeros((own_block.shape[1], partner.shape[1], lag_rows.shape[1]), jnp.float32)
    for offset in range(0, half_len, width):
        crossed = cross_block(own_block, partner, offset, width)
        table_rows = jnp.concatenate(
            [
                lag_rows[offset : offset + width],
                lag_rows[half_len + offset : half_len + offset + width],
            ],
            axis=0,
        )
        running = running + jnp.einsum(
            "mok,kl->mol", crossed, table_rows, preferred_element_type=jnp.float32
        )
    return running


def on_device(record, alive_mask, owners):
    w_dev, sta_dev, samples = record.shape
    half_len = samples // 2
    forward = forward_table(samples, half_len)
    lag_rows = lag_table(samples, half_len, MAXLAG)
    day_pos = lax.axis_index("day")
    sta_pos = lax.axis_index("sta")
    day_count = lax.axis_size("day")
    mask_real = alive_mask.astype(jnp.float32)
    own_cols = lax.dynamic_slice_in_dim(mask_real, sta_pos * sta_dev, sta_dev, 1)
    own_now = lax.dynamic_slice_in_dim(own_cols, day_pos * w_dev, w_dev, 0)
    whitened = whiten(record, own_now, forward)
    src_dev = OWNERS * sta_dev // day_count
    first_src = day_pos * src_dev
    owner_pos = first_src // sta_dev
    offset_src = first_src % sta_dev
    source_col = owners[owner_pos] * sta_dev + offset_src
    source_mask = lax.dynamic_slice_in_dim(mask_real, source_col, src_dev, 1)
    counts = jnp.dot(own_cols.T, source_mask, precision=lax.Precision.HIGHEST)
    blocks = []
    for which in range(OWNERS):
        partner = from_root(whitened, "sta", owners[which])
        blocks.append(cross_lags(whitened, partner, lag_rows))
    correlation = lax.psum_scatter(
        jnp.concatenate(blocks, axis=1), "day", scatter_dimension=1, tiled=True
    )
    return correlation / jnp.sqrt(jnp.maximum(counts, 1.0))[..., None]


def solution(mesh):
    return jax.shard_map(
        on_device,
        mesh=mesh,
        in_specs=(P("day", "sta", None), P(), P()),
        out_specs=P("sta", "day", None),
        check_vma=False,
    )
```

profile of v0, /device:TPU:8, one launch (start us, length us, event | category | flops | bytes accessed | tf_op | source)
XLA Modules:
  0.0 482.9 jit_solution(2637417883073906828)
XLA Ops:
  6.5 1.5 fusion.84
  11.3 8.6 %cosine_convert_fusion = (bf16[1024,512]{1,0:T(8,128)(2,1)S(1)}, bf16[1024,512]{1,0:T(8,128)(2,1)S(1)}) fusion(s32[512]{0:T(512)S(1)} %iota_add_fusion.1), kind=kLoop, calls=%fused_computation.11 | loop fusion | flops 8912896 | bytes 2099200 | tf_op jit(solution)/shard_map/convert_element_type | solution.py:22
  21.6 2.7 multiply_convert_fusion.1
  25.8 266.0 %all-reduce.3.cloned.1.call-done = (bf16[4,8,1024]{2,1,0:T(8,128)(2,1)}, bf16[4,8,1024]{2,1,0:T(8,128)(2,1)}, bf16[4,8,1024]{2,1,0:T(8,128)(2,1)}, bf16[4,8,1024]{2,1,0:T(8,128)(2,1)}) async-done(((bf16[4,8,1024]{2,1,0:T(8,128)(2,1)}, bf16[4,8,1024]{2,1,0:T(8,128)(2,1)}, bf16[4,8,1024]{2,1,0:T(8,128)(2,1)}, bf16[4,8,1024]{2,1,0:T(8,128)(2,1)}), (bf16[4,8,1024]{2,1,0:T(8,128)(2,1)}, ...) | async-done | bytes 262160 | tf_op jit(solution)/shard_map/psum | solution.py:14
  291.8 1.5 fusion.78
  293.6 1.6 fusion.86
  295.7 1.5 fusion.85
  297.7 1.6 copy.15
  300.2 2.5 fusion.89
  302.6 1.5 fusion.91
  304.1 1.5 fusion.90
  305.7 1.5 fusion.92
  308.0 1.5 fusion.93
  309.6 1.5 fusion.95
  311.9 1.5 fusion.94
  313.4 1.5 fusion.96
  315.8 1.5 fusion.97
  317.3 1.5 fusion.99
  318.9 1.5 fusion.98
  320.5 1.5 fusion.100
  323.5 1.5 fusion.101
  325.0 1.5 fusion.103
  327.4 1.5 fusion.102
  328.9 1.5 fusion.104
  331.2 1.5 fusion.105
  332.7 1.5 fusion.107
  335.1 1.7 fusion.106
  336.9 1.5 fusion.108
  339.2 1.5 fusion.113
  340.7 1.5 fusion.115
  343.1 1.5 fusion.114
  344.6 1.5 fusion.116
  346.3 1.5 fusion.110
  347.8 1.5 fusion.112
  349.5 1.5 fusion.109
  351.0 1.5 fusion.111
  352.5 1.6 copy.12
  357.1 2.2 copy.20
  361.3 1.0 copy.24
  362.3 2.2 copy.26
  366.9 2.2 copy.32
  369.1 1.0 copy.33
  372.1 2.2 copy.38
  377.3 2.2 copy.44
  379.5 1.2 copy.45
  382.7 2.2 copy.56
  387.9 1.6 copy.48
  396.3 78.3 %reduce-scatter.2.cloned.1.call-done = f32[8,2,257]{2,0,1:T(8,128)} async-done(((f32[8,32,257]{2,0,1:T(8,128)}), f32[8,2,257]{2,0,1:T(8,128)}) %reduce-scatter.2.cloned.1.call-update) | async-done | bytes 16464 | tf_op jit(solution)/shard_map/reduce_scatter | solution.py:107
  (203 shorter events, 39.7 us)
Async XLA Ops:
  6.5 13.4 %copy-start = (bf16[4,8,1024]{2,1,0:T(8,128)(2,1)S(1)}, bf16[4,8,1024]{2,1,0:T(8,128)(2,1)}, u32[]{:S(2)}) copy-start(bf16[4,8,1024]{2,1,0:T(8,128)(2,1)} %param.3) | copy-start | bytes 196612
  6.5 285.3 %all-reduce.3.cloned.1.call-start = ((), (), s32[]{:S(2)}) async-start(), calls=%async_computation.2 | async-start | bytes 524288 | tf_op jit(solution)/shard_map/psum | solution.py:14
  21.5 453.1 %reduce-scatter.2.cloned.1.call-start = ((), (), s32[]{:S(2)}) async-start(), calls=%async_computation.1 | async-start | bytes 417792 | tf_op jit(solution)/shard_map/reduce_scatter | solution.py:107
  300.1 2.5 copy-start.23
  320.5 1.5 copy-start.55
  320.5 1.5 copy-start.56
  344.6 1.6 copy-start.54
  352.5 1.6 copy-start.3
  354.9 1.2 copy-start.6
  356.1 3.2 copy-start.1
  357.1 3.2 copy-start.4
  359.3 2.0 copy-start.7
  361.3 3.2 copy-start.2
  362.3 3.2 copy-start.8
  364.5 2.0 copy-start.9
  366.5 2.6 copy-start.5
  366.9 3.2 copy-start.10
  369.1 2.0 copy-start.13
  371.1 3.2 copy-start.11
  372.1 3.2 copy-start.14
  374.3 2.0 copy-start.16
  376.3 3.2 copy-start.12
  377.3 3.5 copy-start.17
  379.5 2.2 copy-start.18
  381.7 3.2 copy-start.15
  382.7 3.2 copy-start.19
  385.0 2.0 copy-start.21
  386.9 2.6 copy-start.20
  387.9 2.6 copy-start.22
  389.5 1.5 copy-start.27
  389.6 1.5 copy-start.28
  389.6 1.5 copy-start.33
  390.6 0.9 copy-start.45
  390.6 1.0 copy-start.48
  390.6 1.1 copy-start.52
  390.6 1.1 copy-start.53
  391.0 1.3 copy-start.24
  391.0 1.3 copy-start.25
  391.0 1.3 copy-start.29
  391.1 1.3 copy-start.30
  391.1 1.3 copy-start.35
  391.4 1.0 copy-start.36
  391.4 1.0 copy-start.41
  391.7 0.9 copy-start.31
  392.0 0.9 copy-start.43
  392.0 1.0 copy-start.46
  392.4 1.0 copy-start.50
  392.4 1.0 copy-start.51
  (11 other events, 9.9 us)
Sparse Core Ops, SparseCore 0:
  21.6 270.1 all-reduce.2
  395.6 78.9 reduce-scatter.1
where the time goes:
time: 484 us; the launch traced here: 483 us
  waiting for transfers between devices  344 us (71%)
  local copies, waits for them, and re-layouts  57.6 us (12%)
  matrix products  49.5 us (10%)
  between operations  17.2 us (4%)
  other arithmetic  14.1 us (3%)
    psum x1, waiting for transfers between devices, from_root(): return lax.psum(block, axis)  266 us
    reduce_scatter x1, waiting for transfers between devices, on_device(): lax.psum_scatter(jnp.concatenate(blocks, axis=1), 'day', scatter_dimensio...  78.3 us
    dot_general x8, local copies, waits for them, and re-layouts, cross_block(): jnp.einsum(form, own_imag, par_imag, preferred_element_type=jnp.float32)  16 us
    dot_general x8, matrix products, cross_block(): jnp.einsum(form, own_real, par_real, preferred_element_type=jnp.float32)  12.9 us
    dot_general x8, matrix products, cross_block(): jnp.einsum(form, own_imag, par_imag, preferred_element_type=jnp.float32)  12.3 us
    dot_general x8, matrix products, cross_block(): jnp.einsum(form, own_real, par_imag, preferred_element_type=jnp.float32)  10.9 us
    dot_general x8, matrix products, cross_block(): jnp.einsum(form, own_imag, par_real, preferred_element_type=jnp.float32)  10.9 us
  transfers between devices with their start and end apart: 2, of which 2 were waited for; matrix products, arithmetic and copies ran while one was open for 1% of the time, Pallas kernels for 0%

commit v1 on v0

v1 whole, which is shorter than its diff:
```python
import math

import jax
import jax.numpy as jnp
import numpy as np
from jax import lax
from jax.experimental import pallas as pl
from jax.experimental.pallas import tpu as pltpu
from jax.sharding import PartitionSpec as P

MAXLAG = 128
OWNERS = 4
LANES = 384
SHARE = 4


def forward_table(samples, half_len):
    times = np.arange(samples)[:, None]
    bins = np.arange(1, half_len + 1)[None, :]
    phase = (times * bins % samples).astype(np.float32) * np.float32(2.0 * math.pi / samples)
    return np.concatenate([np.cos(phase), -np.sin(phase)], axis=1).astype(jnp.bfloat16)


def lag_table(samples, half_len, reach):
    bins = np.arange(1, half_len + 1)[:, None]
    shifts = np.arange(-reach, reach + 1)[None, :]
    phase = (bins * shifts % samples).astype(np.float32) * np.float32(2.0 * math.pi / samples)
    weight = (np.where(bins == half_len, 1.0, 2.0) / math.sqrt(samples)).astype(np.float32)
    table = np.concatenate([weight * np.cos(phase), -weight * np.sin(phase)], axis=0)
    return np.pad(table, ((0, 0), (0, LANES - table.shape[1]))).astype(jnp.bfloat16)


def owner_columns(owners_ref, rows, source, width):
    block = source // width
    owner = jnp.zeros_like(source)
    for which in range(OWNERS):
        owner = jnp.where(block == which, owners_ref[which], owner)
    return owner * width + lax.rem(source, width)


def pick_rows(columns, mask_ref):
    stations = lax.broadcasted_iota(jnp.int32, columns.shape, 1)
    chosen = jnp.where(stations == columns, 1.0, 0.0).astype(jnp.bfloat16)
    mask = mask_ref[...].astype(jnp.float32).astype(jnp.bfloat16)
    return lax.dot_general(
        chosen, mask, (((1,), (1,)), ((), ())), preferred_element_type=jnp.float32
    )


def whiten(rows, forward_ref, masks):
    half_len = forward_ref.shape[1] // 2
    spectrum = jnp.dot(rows, forward_ref[...], preferred_element_type=jnp.float32)
    real_part = spectrum[:, :half_len]
    imag_part = spectrum[:, half_len:]
    magnitude = jnp.sqrt(real_part * real_part + imag_part * imag_part)
    level = jnp.mean(magnitude, axis=-1, keepdims=True)
    factor = masks / (magnitude + 0.3 * level + 1e-06)
    return (
        (real_part * factor).astype(jnp.bfloat16).astype(jnp.float32),
        (imag_part * factor).astype(jnp.bfloat16).astype(jnp.float32),
    )


def cross_kernel(
    place_ref, owners_ref, own_ref, src_ref, mask_ref, forward_ref, lag_ref, out_ref, src_re, src_im
):
    first_window, sta_pos = place_ref[0], place_ref[1]
    sources = src_ref.shape[0] // SHARE
    width = own_ref.shape[0] // SHARE
    stations = mask_ref.shape[1]
    both = sources + width
    row = lax.broadcasted_iota(jnp.int32, (both, stations), 0)
    columns = jnp.where(
        row < sources,
        owner_columns(owners_ref, both, row, width),
        sta_pos * width + row - sources,
    )
    alive = pick_rows(columns, mask_ref)
    window = lax.broadcasted_iota(jnp.int32, alive.shape, 1)
    now = [
        jnp.sum(jnp.where(window == first_window + w, alive, 0.0), axis=1, keepdims=True)
        for w in range(SHARE)
    ]
    src_masks = jnp.concatenate([m[:sources] for m in now], axis=0)
    own_masks = jnp.concatenate([m[sources:] for m in now], axis=0)
    own_re, own_im = whiten(own_ref[...], forward_ref, own_masks)
    src_re[...], src_im[...] = whiten(src_ref[...], forward_ref, src_masks)
    half_len = own_re.shape[1]
    crossed = []
    for source in range(sources):
        real_sum = jnp.zeros((width, half_len), jnp.float32)
        imag_sum = jnp.zeros((width, half_len), jnp.float32)
        for w in range(SHARE):
            at = w * sources + source
            re, im = src_re[at : at + 1, :], src_im[at : at + 1, :]
            mine_re = own_re[w * width : (w + 1) * width]
            mine_im = own_im[w * width : (w + 1) * width]
            real_sum = real_sum + (mine_re * re + mine_im * im)
            imag_sum = imag_sum + (mine_im * re - mine_re * im)
        crossed.append(jnp.concatenate([real_sum, imag_sum], axis=1))
    for first in range(0, sources, 16):
        block = jnp.concatenate(crossed[first : first + 16], axis=0).astype(jnp.bfloat16)
        out_ref[first * width : (first + 16) * width, :] = jnp.dot(
            block, lag_ref[...], preferred_element_type=jnp.float32
        ).astype(out_ref.dtype)


def final_kernel(place_ref, owners_ref, parts_ref, mask_ref, out_ref):
    first_source, sta_pos = place_ref[0], place_ref[1]
    width, src_dev, lags = out_ref.shape
    rows = width * src_dev
    stations = mask_ref.shape[1]
    row = lax.broadcasted_iota(jnp.int32, (2 * rows, stations), 0)
    source = first_source + lax.rem(row, rows) // width
    columns = jnp.where(
        row < rows,
        sta_pos * width + lax.rem(row, width),
        owner_columns(owners_ref, 2 * rows, source, width),
    )
    alive = pick_rows(columns, mask_ref)
    counts = jnp.sum(alive[:rows] * alive[rows:], axis=1, keepdims=True)
    total = parts_ref[0:rows, :].astype(jnp.float32)
    for part in range(1, parts_ref.shape[0] // rows):
        total = total + parts_ref[part * rows : (part + 1) * rows, :].astype(jnp.float32)
    total = total / jnp.sqrt(jnp.maximum(counts, 1.0))
    for which in range(src_dev):
        out_ref[:, which, :] = total[which * width : (which + 1) * width, :lags]


def in_vmem():
    return pl.BlockSpec(memory_space=pltpu.VMEM)


def in_smem():
    return pl.BlockSpec(memory_space=pltpu.SMEM)


def on_device(record, alive_mask, owners):
    w_dev, sta_dev, samples = record.shape
    half_len = samples // 2
    sources = OWNERS * sta_dev
    forward = jnp.asarray(forward_table(samples, half_len))
    lag_rows = jnp.asarray(lag_table(samples, half_len, MAXLAG))
    day_count, sta_count = lax.axis_size("day"), lax.axis_size("sta")
    day_pos, sta_pos = lax.axis_index("day"), lax.axis_index("sta")
    src_dev = sources // day_count

    spread = jnp.broadcast_to(
        record.reshape(1, 2, 1, 2, sta_dev, samples),
        (sta_count // 8, 2, 2, 2, sta_dev, samples),
    ).reshape(sta_count, sta_dev, samples)
    everyone = lax.all_to_all(spread, "sta", 0, 0)
    chosen = jnp.concatenate(
        [lax.dynamic_slice_in_dim(everyone, owners[which], 1, 0) for which in range(OWNERS)], axis=0
    )
    quads = [
        [8 * pair + 4 * odd + 2 * far + core for odd in range(2) for core in range(2)]
        for pair in range(sta_count // 8)
        for far in range(2)
    ]
    gathered = lax.all_gather(chosen, "sta", axis_index_groups=quads)

    pieces = pl.pallas_call(
        cross_kernel,
        out_shape=jax.ShapeDtypeStruct((sources * sta_dev, LANES), jnp.bfloat16),
        in_specs=[in_smem(), in_smem()] + [in_vmem()] * 5,
        out_specs=in_vmem(),
        scratch_shapes=[pltpu.VMEM((w_dev * sources, half_len), jnp.float32)] * 2,
        compiler_params=pltpu.CompilerParams(vmem_limit_bytes=24 * 2**20),
        name="cross_lags",
    )(
        jnp.stack([day_pos * w_dev, sta_pos]).astype(jnp.int32),
        owners,
        record.reshape(w_dev * sta_dev, samples),
        gathered.reshape(w_dev * sources, samples),
        alive_mask,
        forward,
        lag_rows,
    )
    rows = src_dev * sta_dev
    parts = lax.all_to_all(pieces.reshape(day_count, rows, LANES), "day", 0, 0)
    return pl.pallas_call(
        final_kernel,
        out_shape=jax.ShapeDtypeStruct((sta_dev, src_dev, 2 * MAXLAG + 1), jnp.float32),
        in_specs=[in_smem(), in_smem()] + [in_vmem()] * 2,
        out_specs=in_vmem(),
        compiler_params=pltpu.CompilerParams(vmem_limit_bytes=16 * 2**20),
        name="sum_parts",
    )(
        jnp.stack([day_pos * src_dev, sta_pos]).astype(jnp.int32),
        owners,
        parts.reshape(day_count * rows, LANES),
        alive_mask,
    )


def solution(mesh):
    return jax.shard_map(
        on_device,
        mesh=mesh,
        in_specs=(P("day", "sta", None), P(), P()),
        out_specs=P("sta", "day", None),
        check_vma=False,
    )
```

time: 484 us -> 63.9 us (0.13)
  the two profiles are of different devices: /device:TPU:8 before, /device:TPU:4 now
where the time goes in v1:
time: 63.9 us; the launch traced here: 63.4 us
  starting transfers between devices  21.3 us (33%)
  waiting for transfers between devices  19.9 us (31%)
  between operations  7.47 us (12%)
  blocking collectives  5.79 us (9%)
  local copies, waits for them, and re-layouts  4.45 us (7%)
  Pallas kernels  4.33 us (7%)
    all_to_all x1, waiting for transfers between devices, on_device(): parts = lax.all_to_all(pieces.reshape(day_count, rows, LANES), 'day', 0, 0)  11.2 us
    all_to_all x1, starting transfers between devices, on_device(): parts = lax.all_to_all(pieces.reshape(day_count, rows, LANES), 'day', 0, 0)  11.1 us
    all_to_all x1, starting transfers between devices, on_device(): everyone = lax.all_to_all(spread, 'sta', 0, 0)  10.2 us
    all_to_all x1, waiting for transfers between devices, on_device(): everyone = lax.all_to_all(spread, 'sta', 0, 0)  8.75 us
    all_gather x1, blocking collectives, on_device(): gathered = lax.all_gather(chosen, 'sta', axis_index_groups=quads)  5.79 us
    pallas_call x1, Pallas kernels, on_device(): pl.pallas_call(cross_kernel, out_shape=jax.ShapeDtypeStruct((sources * st...  2.95 us
    broadcast_in_dim x1, local copies, waits for them, and re-layouts, on_device(): jnp.broadcast_to(record.reshape(1, 2, 1, 2, sta_dev, samples), (sta_count...  1.84 us
    slice x1, local copies, waits for them, and re-layouts, on_device(): owners[which]  1.46 us
  transfers between devices with their start and end apart: 2, of which 2 were waited for; matrix products, arithmetic and copies ran while one was open for 3% of the time, Pallas kernels for 0%

profile of v1, /device:TPU:4, one launch (start us, length us, event | category | flops | bytes accessed | tf_op | source)
XLA Modules:
  0.0 63.4 jit_solution(5703130653512542007)
XLA Ops:
  0.0 0.0 copy-start
  0.0 0.0 copy-start.2
  0.0 0.0 copy-start.4
  0.0 0.0 copy-start.3
  0.0 1.8 %broadcast_in_dim.8 = bf16[4,2,2,2,8,1024]{5,4,3,2,1,0:T(8,128)(2,1)} broadcast(bf16[2,2,8,1024]{3,2,1,0:T(8,128)(2,1)} %bitcast.15), dimensions={1,3,4,5} | broadcast | bytes 589824 | tf_op jit(solution)/shard_map/broadcast_in_dim | solution.py:148
  1.9 10.2 %all-to-all-start = ((bf16[32,8,1024]{2,1,0:T(8,128)(2,1)}), bf16[32,8,1024]{2,1,0:T(8,128)(2,1)S(1)}, u32[]{:S(2)}, u32[]{:S(2)}) async-start(bf16[32,8,1024]{2,1,0:T(8,128)(2,1)} %bitcast.5), calls=%async_computation | async-start | bytes 1048576 | tf_op jit(solution)/shard_map/all_to_all | solution.py:152
  12.1 1.5 %fusion = (s32[1]{0:T(128)}, s32[1]{0:T(128)}, s32[1]{0:T(128)}, s32[1]{0:T(128)}) fusion(s32[4]{0:T(128)} %owners_ref.3), kind=kLoop, calls=%fused_computation.7 | loop fusion | bytes 32 | tf_op jit(solution)/shard_map/slice | solution.py:154
  21.0 0.1 pad_add_fusion.1.place_ref
  21.0 8.8 %all-to-all-done = bf16[32,8,1024]{2,1,0:T(8,128)(2,1)S(1)} async-done(((bf16[32,8,1024]{2,1,0:T(8,128)(2,1)}), bf16[32,8,1024]{2,1,0:T(8,128)(2,1)S(1)}, u32[]{:S(2)}, u32[]{:S(2)}) %all-to-all-start) | async-done | bytes 524320 | tf_op jit(solution)/shard_map/all_to_all | solution.py:152
  29.8 5.8 %all-gather = bf16[16,8,1024]{2,1,0:T(8,128)(2,1)S(1)} all-gather(bf16[4,8,1024]{2,1,0:T(8,128)(2,1)S(1)} %pad_maximum_fusion), channel_id=2, replica_groups={{0,1,4,5},{2,3,6,7},{8,9,12,13},{10,11,14,15},{16,17,20,21},{18,19,22,2..., dimensions={0}, use_global_device_ids=true | all-gather | bytes 327680 | tf_op jit(solution)/shard_map/all_gather | solution.py:161
  35.6 0.0 copy-done
  35.6 0.0 copy-done.2
  35.6 0.0 copy-done.4
  35.6 0.0 copy-done.3
  35.6 0.0 copy-start.1
  35.6 1.1 %copy-done.1 = bf16[1024,384]{1,0:T(8,128)(2,1)S(1)} copy-done((bf16[1024,384]{1,0:T(8,128)(2,1)S(1)}, bf16[1024,384]{1,0:T(8,128)(2,1)}, u32[]{:S(2)}) %copy-start.1) | copy-done | bytes 786456
  36.8 2.9 %cross_lags.1 = bf16[256,384]{1,0:T(8,128)(2,1)} custom-call(s32[2]{0:T(128)S(1)} %pad_add_fusion.1.place_ref, s32[4]{0:T(128)S(1)} %copy-done.4, bf16[32,1024]{1,0:T(8,128)(2,1)S(1)} %bitcast.16, bf16[128,1024]{1,0:T(8,128)(2,1)S(1)} %bitcast.13, s32[64,256]{1,0:T(8,128)S(1)} %copy-done.3, bf16[1024,1024]{1,0:T(8,128)(2,1)S(1)} %copy-done, ...), custom_call_target="tpu_custom_call" | custom-call | tf_op jit(solution)/shard_map/cross_lags/pallas_call | solution.py:163
  39.7 11.1 %all-to-all-start.1 = ((bf16[16,16,384]{2,1,0:T(8,128)(2,1)}), bf16[16,16,384]{2,1,0:T(8,128)(2,1)S(1)}, u32[]{:S(2)}, u32[]{:S(2)}) async-start(bf16[16,16,384]{2,1,0:T(8,128)(2,1)} %bitcast.11), calls=%async_computation.1 | async-start | bytes 393216 | tf_op jit(solution)/shard_map/all_to_all | solution.py:181
  50.8 0.1 pad_add_fusion.place_ref
  50.8 11.2 %all-to-all-done.1 = bf16[16,16,384]{2,1,0:T(8,128)(2,1)S(1)} async-done(((bf16[16,16,384]{2,1,0:T(8,128)(2,1)}), bf16[16,16,384]{2,1,0:T(8,128)(2,1)S(1)}, u32[]{:S(2)}, u32[]{:S(2)}) %all-to-all-start.1) | async-done | bytes 196640 | tf_op jit(solution)/shard_map/all_to_all | solution.py:181
  62.0 1.4 %sum_parts.1 = f32[8,2,257]{2,1,0:T(2,128)} custom-call(s32[2]{0:T(128)S(1)} %pad_add_fusion.place_ref, s32[4]{0:T(128)S(1)} %copy-done.4, bf16[256,384]{1,0:T(8,128)(2,1)S(1)} %bitcast.14, s32[64,256]{1,0:T(8,128)S(1)} %copy-done.3), custom_call_target="tpu_custom_call" | custom-call | tf_op jit(solution)/shard_map/sum_parts/pallas_call | solution.py:182
  (2 shorter events, 0.0 us)
Async XLA Ops:
  0.0 35.6 %copy-start = (bf16[1024,1024]{1,0:T(8,128)(2,1)S(1)}, bf16[1024,1024]{1,0:T(8,128)(2,1)}, u32[]{:S(2)}) copy-start(bf16[1024,1024]{1,0:T(8,128)(2,1)} %constant.21.clone.forward_ref) | copy-start | bytes 6291460
  0.0 35.6 %copy-start.2 = (bf16[4,8,1024]{2,1,0:T(8,128)(2,1)S(1)}, bf16[4,8,1024]{2,1,0:T(8,128)(2,1)}, u32[]{:S(2)}) copy-start(bf16[4,8,1024]{2,1,0:T(8,128)(2,1)} %param.5) | copy-start | bytes 196612
  0.0 35.6 %copy-start.4 = (s32[4]{0:T(128)S(1)}, s32[4]{0:T(128)}, u32[]{:S(2)}) copy-start(s32[4]{0:T(128)} %owners_ref.3) | copy-start | bytes 52
  0.0 35.6 %copy-start.3 = (s32[64,256]{1,0:T(8,128)S(1)}, s32[64,256]{1,0:T(8,128)}, u32[]{:S(2)}) copy-start(s32[64,256]{1,0:T(8,128)} %mask_ref.3) | copy-start | bytes 196612
  1.9 27.9 %all-to-all-start = ((bf16[32,8,1024]{2,1,0:T(8,128)(2,1)}), bf16[32,8,1024]{2,1,0:T(8,128)(2,1)S(1)}, u32[]{:S(2)}, u32[]{:S(2)}) async-start(bf16[32,8,1024]{2,1,0:T(8,128)(2,1)} %bitcast.5), calls=%async_computation | async-start | bytes 1048576 | tf_op jit(solution)/shard_map/all_to_all | solution.py:152
  35.6 1.1 %copy-start.1 = (bf16[1024,384]{1,0:T(8,128)(2,1)S(1)}, bf16[1024,384]{1,0:T(8,128)(2,1)}, u32[]{:S(2)}) copy-start(bf16[1024,384]{1,0:T(8,128)(2,1)} %constant.22.clone.lag_ref) | copy-start | bytes 2359300
  39.7 22.3 %all-to-all-start.1 = ((bf16[16,16,384]{2,1,0:T(8,128)(2,1)}), bf16[16,16,384]{2,1,0:T(8,128)(2,1)S(1)}, u32[]{:S(2)}, u32[]{:S(2)}) async-start(bf16[16,16,384]{2,1,0:T(8,128)(2,1)} %bitcast.11), calls=%async_computation.1 | async-start | bytes 393216 | tf_op jit(solution)/shard_map/all_to_all | solution.py:181

commit v2 on v1

v2 whole, which is shorter than its diff:
```python
import math

import jax
import jax.numpy as jnp
import numpy as np
from jax import lax
from jax.experimental import pallas as pl
from jax.experimental.pallas import tpu as pltpu
from jax.sharding import PartitionSpec as P

MAXLAG = 128
OWNERS = 4
LANES = 384
SHARE = 4


def forward_table(samples, half_len):
    times = np.arange(samples)[:, None]
    bins = np.arange(1, half_len + 1)[None, :]
    phase = (times * bins % samples).astype(np.float32) * np.float32(2.0 * math.pi / samples)
    return np.concatenate([np.cos(phase), -np.sin(phase)], axis=1).astype(jnp.bfloat16)


def lag_table(samples, half_len, reach):
    bins = np.arange(1, half_len + 1)[:, None]
    shifts = np.arange(-reach, reach + 1)[None, :]
    phase = (bins * shifts % samples).astype(np.float32) * np.float32(2.0 * math.pi / samples)
    weight = (np.where(bins == half_len, 1.0, 2.0) / math.sqrt(samples)).astype(np.float32)
    table = np.concatenate([weight * np.cos(phase), -weight * np.sin(phase)], axis=0)
    return np.pad(table, ((0, 0), (0, LANES - table.shape[1]))).astype(jnp.bfloat16)


def owner_columns(owners_ref, source, width):
    block = source // width
    owner = jnp.zeros_like(source)
    for which in range(OWNERS):
        owner = jnp.where(block == which, owners_ref[which], owner)
    return owner * width + lax.rem(source, width)


def pick_rows(columns, mask_ref):
    stations = lax.broadcasted_iota(jnp.int32, columns.shape, 1)
    chosen = jnp.where(stations == columns, 1.0, 0.0).astype(jnp.bfloat16)
    mask = mask_ref[...].astype(jnp.float32).astype(jnp.bfloat16)
    return lax.dot_general(
        chosen, mask, (((1,), (1,)), ((), ())), preferred_element_type=jnp.float32
    )


def whiten(rows, forward_ref, masks):
    half_len = forward_ref.shape[1] // 2
    spectrum = jnp.dot(rows, forward_ref[...], preferred_element_type=jnp.float32)
    real_part = spectrum[:, :half_len]
    imag_part = spectrum[:, half_len:]
    magnitude = jnp.sqrt(real_part * real_part + imag_part * imag_part)
    level = jnp.mean(magnitude, axis=-1, keepdims=True)
    factor = masks / (magnitude + 0.3 * level + 1e-06)
    return (
        (real_part * factor).astype(jnp.bfloat16).astype(jnp.float32),
        (imag_part * factor).astype(jnp.bfloat16).astype(jnp.float32),
    )


def prepare_kernel(
    place_ref, owners_ref, own_ref, mask_ref, forward_ref, white_ref, masks_ref, scale_ref
):
    day_pos, sta_pos = place_ref[0], place_ref[1]
    sources = masks_ref.shape[0] // SHARE
    width = own_ref.shape[0] // SHARE
    stations = mask_ref.shape[1]
    rows = scale_ref.shape[0]
    src_dev = rows // width
    first_window = day_pos * SHARE
    row = lax.broadcasted_iota(jnp.int32, (sources + 2 * rows, stations), 0)
    last = row - sources - rows
    columns = jnp.where(
        row < sources,
        owner_columns(owners_ref, row, width),
        jnp.where(
            last < 0,
            sta_pos * width + lax.rem(row - sources, width),
            owner_columns(owners_ref, day_pos * src_dev + last // width, width),
        ),
    )
    alive = pick_rows(columns, mask_ref)
    window = lax.broadcasted_iota(jnp.int32, alive.shape, 1)
    now = [
        jnp.sum(jnp.where(window == first_window + w, alive, 0.0), axis=1, keepdims=True)
        for w in range(SHARE)
    ]
    for w in range(SHARE):
        masks_ref[w * sources : (w + 1) * sources, :] = jnp.broadcast_to(
            now[w][:sources], (sources, masks_ref.shape[1])
        )
    own_masks = jnp.concatenate([m[sources : sources + width] for m in now], axis=0)
    real_part, imag_part = whiten(own_ref[...], forward_ref, own_masks)
    white_ref[...] = jnp.concatenate([real_part, imag_part], axis=1)
    counts = jnp.sum(
        alive[sources : sources + rows] * alive[sources + rows :], axis=1, keepdims=True
    )
    scale_ref[...] = jnp.broadcast_to(1.0 / jnp.sqrt(jnp.maximum(counts, 1.0)), scale_ref.shape)


def cross_kernel(
    white_ref, tiles_ref, masks_ref, forward_ref, lag_hbm, out_ref, src_re, src_im, lag_ref, sem
):
    fetch = pltpu.make_async_copy(lag_hbm, lag_ref, sem)
    fetch.start()
    sources = masks_ref.shape[0] // SHARE
    width = white_ref.shape[0] // SHARE
    half_len = src_re.shape[1]
    tiles = tiles_ref.shape[0] // sources
    wide = tiles // SHARE
    rows = []
    for w in range(SHARE):
        at = [(t % 2) * (tiles // 2) + t // 2 for t in range(w * wide, (w + 1) * wide)]
        rows.append(
            jnp.concatenate([tiles_ref[a * sources : (a + 1) * sources, :] for a in at], axis=1)
        )
    src_re[...], src_im[...] = whiten(
        jnp.concatenate(rows, axis=0), forward_ref, masks_ref[:, 0:1]
    )
    crossed = []
    for source in range(sources):
        real_sum = jnp.zeros((width, half_len), jnp.float32)
        imag_sum = jnp.zeros((width, half_len), jnp.float32)
        for w in range(SHARE):
            at = w * sources + source
            re, im = src_re[at : at + 1, :], src_im[at : at + 1, :]
            mine_re = white_ref[w * width : (w + 1) * width, :half_len]
            mine_im = white_ref[w * width : (w + 1) * width, half_len:]
            real_sum = real_sum + (mine_re * re + mine_im * im)
            imag_sum = imag_sum + (mine_im * re - mine_re * im)
        crossed.append(jnp.concatenate([real_sum, imag_sum], axis=1))
    fetch.wait()
    for first in range(0, sources, 16):
        block = jnp.concatenate(crossed[first : first + 16], axis=0).astype(jnp.bfloat16)
        out_ref[first * width : (first + 16) * width, :] = jnp.dot(
            block, lag_ref[...], preferred_element_type=jnp.float32
        ).astype(out_ref.dtype)


def final_kernel(parts_ref, scale_ref, out_ref):
    width, src_dev, lags = out_ref.shape
    rows = width * src_dev
    total = parts_ref[0:rows, :].astype(jnp.float32)
    for part in range(1, parts_ref.shape[0] // rows):
        total = total + parts_ref[part * rows : (part + 1) * rows, :].astype(jnp.float32)
    total = total * scale_ref[:, 0:1]
    for which in range(src_dev):
        out_ref[:, which, :] = total[which * width : (which + 1) * width, :lags]


def in_vmem():
    return pl.BlockSpec(memory_space=pltpu.VMEM)


def in_smem():
    return pl.BlockSpec(memory_space=pltpu.SMEM)


def on_device(record, alive_mask, owners):
    w_dev, sta_dev, samples = record.shape
    half_len = samples // 2
    sources = OWNERS * sta_dev
    forward = jnp.asarray(forward_table(samples, half_len))
    lag_rows = jnp.asarray(lag_table(samples, half_len, MAXLAG))
    day_count, sta_count = lax.axis_size("day"), lax.axis_size("sta")
    day_pos, sta_pos = lax.axis_index("day"), lax.axis_index("sta")
    src_dev = sources // day_count
    rows = src_dev * sta_dev
    place = jnp.stack([day_pos, sta_pos]).astype(jnp.int32)

    tiles = record.reshape(w_dev, sta_dev, sta_count // w_dev, -1)
    tiles = tiles.transpose(0, 2, 1, 3).reshape(sta_count, sta_dev, -1)
    everyone = lax.all_to_all(tiles, "sta", 0, 0)

    white, masks, scale = pl.pallas_call(
        prepare_kernel,
        out_shape=[
            jax.ShapeDtypeStruct((w_dev * sta_dev, samples), jnp.float32),
            jax.ShapeDtypeStruct((w_dev * sources, 128), jnp.float32),
            jax.ShapeDtypeStruct((rows, 128), jnp.float32),
        ],
        in_specs=[in_smem(), in_smem()] + [in_vmem()] * 3,
        out_specs=[in_vmem()] * 3,
        compiler_params=pltpu.CompilerParams(vmem_limit_bytes=16 * 2**20),
        cost_estimate=pl.CostEstimate(
            flops=2 * w_dev * sta_dev * samples * samples,
            bytes_accessed=2 * samples * samples,
            transcendentals=w_dev * sta_dev * samples,
        ),
        name="prepare",
    )(place, owners, record.reshape(w_dev * sta_dev, samples), alive_mask, forward)

    chosen = jnp.concatenate(
        [lax.dynamic_slice_in_dim(everyone, owners[which], 1, 0) for which in range(OWNERS)], axis=0
    )
    cores = [[2 * chip + core for chip in range(sta_count // 2)] for core in range(2)]
    pairs = [[2 * chip, 2 * chip + 1] for chip in range(sta_count // 2)]
    half = lax.all_to_all(
        jnp.broadcast_to(chosen[None], (sta_count // 2,) + chosen.shape),
        "sta", 0, 0, axis_index_groups=cores,
    )
    gathered = lax.all_gather(half, "sta", axis_index_groups=pairs)

    pieces = pl.pallas_call(
        cross_kernel,
        out_shape=jax.ShapeDtypeStruct((sources * sta_dev, LANES), jnp.bfloat16),
        in_specs=[in_vmem()] * 4 + [pl.BlockSpec(memory_space=pl.ANY)],
        out_specs=in_vmem(),
        scratch_shapes=[pltpu.VMEM((w_dev * sources, half_len), jnp.float32)] * 2
        + [pltpu.VMEM((samples, LANES), jnp.bfloat16), pltpu.SemaphoreType.DMA],
        compiler_params=pltpu.CompilerParams(vmem_limit_bytes=24 * 2**20),
        name="cross_lags",
    )(white, gathered.reshape(sta_count * sources, -1), masks, forward, lag_rows)
    parts = lax.all_to_all(pieces.reshape(day_count, rows, LANES), "day", 0, 0)
    return pl.pallas_call(
        final_kernel,
        out_shape=jax.ShapeDtypeStruct((sta_dev, src_dev, 2 * MAXLAG + 1), jnp.float32),
        in_specs=[in_vmem()] * 2,
        out_specs=in_vmem(),
        compiler_params=pltpu.CompilerParams(vmem_limit_bytes=16 * 2**20),
        name="sum_parts",
    )(parts.reshape(day_count * rows, LANES), scale)


def solution(mesh):
    return jax.shard_map(
        on_device,
        mesh=mesh,
        in_specs=(P("day", "sta", None), P(), P()),
        out_specs=P("sta", "day", None),
        check_vma=False,
    )
```

time: 63.9 us -> 67.3 us (1.053)
  the two profiles are of different devices: /device:TPU:4 before, /device:TPU:2 now
where the time goes in v2:
time: 67.3 us; the launch traced here: 66.7 us
  blocking collectives  23.7 us (35%)
  starting transfers between devices  17.4 us (26%)
  waiting for transfers between devices  7.47 us (11%)
  between operations  7.47 us (11%)
  local copies, waits for them, and re-layouts  7.16 us (11%)
  Pallas kernels  3.45 us (5%)
    all_to_all x1, blocking collectives, on_device(): parts = lax.all_to_all(pieces.reshape(day_count, rows, LANES), 'day', 0, 0)  21.7 us
    all_to_all x1, starting transfers between devices, on_device(): everyone = lax.all_to_all(tiles, 'sta', 0, 0)  9.05 us
    all_to_all x1, starting transfers between devices, on_device(): lax.all_to_all(jnp.broadcast_to(chosen[None], (sta_count // 2,) + chosen....  8.38 us
    all_to_all x1, waiting for transfers between devices, on_device(): lax.all_to_all(jnp.broadcast_to(chosen[None], (sta_count // 2,) + chosen....  6.32 us
    unnamed x12, local copies, waits for them, and re-layouts  5.06 us
    all_gather x1, blocking collectives, on_device(): gathered = lax.all_gather(half, 'sta', axis_index_groups=pairs)  1.98 us
    pallas_call x1, Pallas kernels, on_device(): pl.pallas_call(cross_kernel, out_shape=jax.ShapeDtypeStruct((sources * st...  1.68 us
    slice x1, local copies, waits for them, and re-layouts, on_device(): owners[which]  1.42 us
  transfers between devices with their start and end apart: 2, of which 2 were waited for; matrix products, arithmetic and copies ran while one was open for 2% of the time, Pallas kernels for 2%

profile of v2, /device:TPU:2, one launch (start us, length us, event | category | flops | bytes accessed | tf_op | source)
XLA Modules:
  0.0 66.7 jit_solution(9021166385490625911)
XLA Ops:
  0.0 9.1 %all-to-all-start = ((bf16[32,8,128]{2,1,0:T(8,128)(2,1)}), bf16[32,8,128]{2,1,0:T(8,128)(2,1)S(1)}, u32[]{:S(2)}, u32[]{:S(2)}) async-start(bf16[32,8,128]{2,1,0:T(8,128)(2,1)} %bitcast.18), calls=%async_computation | async-start | bytes 131072 | tf_op jit(solution)/shard_map/all_to_all | solution.py:176
  9.1 1.4 %fusion = (s32[1]{0:T(128)}, s32[1]{0:T(128)}, s32[1]{0:T(128)}, s32[1]{0:T(128)}) fusion(s32[4]{0:T(128)} %owners_ref.1), kind=kLoop, calls=%fused_computation.6 | loop fusion | bytes 32 | tf_op jit(solution)/shard_map/slice | solution.py:197
  17.9 1.1 %all-to-all-done = bf16[32,8,128]{2,1,0:T(8,128)(2,1)S(1)} async-done(((bf16[32,8,128]{2,1,0:T(8,128)(2,1)}), bf16[32,8,128]{2,1,0:T(8,128)(2,1)S(1)}, u32[]{:S(2)}, u32[]{:S(2)}) %all-to-all-start) | async-done | bytes 65568 | tf_op jit(solution)/shard_map/all_to_all | solution.py:176
  19.1 0.7 %broadcast_in_dim.2 = bf16[16,4,8,128]{3,2,1,0:T(8,128)(2,1)} broadcast(bf16[4,8,128]{2,1,0:T(8,128)(2,1)S(1)} %pad_maximum_fusion), dimensions={1,2,3} | broadcast | bytes 139264 | tf_op jit(solution)/shard_map/broadcast_in_dim | solution.py:202
  19.7 8.4 %all-to-all-start.1 = ((bf16[16,4,8,128]{3,2,1,0:T(8,128)(2,1)}), bf16[16,4,8,128]{3,2,1,0:T(8,128)(2,1)S(1)}, u32[]{:S(2)}, u32[]{:S(2)}) async-start(bf16[16,4,8,128]{3,2,1,0:T(8,128)(2,1)} %broadcast_in_dim.2), calls=%async_computation.1 | async-start | bytes 262144 | tf_op jit(solution)/shard_map/all_to_all | solution.py:201
  28.1 0.1 pad_add_fusion.place_ref
  28.2 0.0 copy-start
  28.2 1.6 %copy-done = bf16[1024,1024]{1,0:T(8,128)(2,1)S(1)} copy-done((bf16[1024,1024]{1,0:T(8,128)(2,1)S(1)}, bf16[1024,1024]{1,0:T(8,128)(2,1)}, u32[]{:S(2)}) %copy-start) | copy-done | bytes 2097176
  29.8 0.0 copy-start.3
  29.8 0.8 %copy-done.3 = bf16[4,8,1024]{2,1,0:T(8,128)(2,1)S(1)} copy-done((bf16[4,8,1024]{2,1,0:T(8,128)(2,1)S(1)}, bf16[4,8,1024]{2,1,0:T(8,128)(2,1)}, u32[]{:S(2)}) %copy-start.3) | copy-done | bytes 65560
  30.6 0.0 copy-start.4
  30.6 0.8 %copy-done.4 = s32[64,256]{1,0:T(8,128)S(1)} copy-done((s32[64,256]{1,0:T(8,128)S(1)}, s32[64,256]{1,0:T(8,128)}, u32[]{:S(2)}) %copy-start.4) | copy-done | bytes 65560
  31.5 0.0 copy-start.5
  31.5 0.7 copy-done.5
  32.1 0.0 copy-start.1
  32.1 1.1 %prepare.1 = (f32[32,1024]{1,0:T(8,128)S(1)}, f32[128,128]{1,0:T(8,128)S(1)}, f32[16,128]{1,0:T(8,128)S(1)}) custom-call(s32[2]{0:T(128)S(1)} %pad_add_fusion.place_ref, s32[4]{0:T(128)S(1)} %copy-done.5, bf16[32,1024]{1,0:T(8,128)(2,1)S(1)} %bitcast.19, s32[64,256]{1,0:T(8,128)S(1)} %copy-done.4, bf16[1024,1024]{1,0:T(8,128)(2,1)S(1)} %copy-done), custom_call_target="tpu_custom_call" | custom-call | flops 67108864 | bytes 2097152 | tf_op jit(solution)/shard_map/prepare/pallas_call | solution.py:178
  33.2 6.3 %all-to-all-done.1 = bf16[16,4,8,128]{3,2,1,0:T(8,128)(2,1)S(1)} async-done(((bf16[16,4,8,128]{3,2,1,0:T(8,128)(2,1)}), bf16[16,4,8,128]{3,2,1,0:T(8,128)(2,1)S(1)}, u32[]{:S(2)}, u32[]{:S(2)}) %all-to-all-start.1) | async-done | bytes 131104 | tf_op jit(solution)/shard_map/all_to_all | solution.py:201
  39.5 2.0 %all-gather = bf16[32,4,8,128]{3,2,1,0:T(8,128)(2,1)S(1)} all-gather(bf16[16,4,8,128]{3,2,1,0:T(8,128)(2,1)S(1)} %all-to-all-done.1), channel_id=2, replica_groups={{0,1},{2,3},{4,5},{6,7},{8,9},{10,11},{12,13},{14,15},{16,17},{18,19},{..., dimensions={0}, use_global_device_ids=true | all-gather | bytes 393216 | tf_op jit(solution)/shard_map/all_gather | solution.py:205
  41.5 0.0 copy-done.1
  41.5 0.0 copy-start.2
  41.5 1.1 %copy-done.2 = bf16[1024,384]{1,0:T(8,128)(2,1)S(1)} copy-done((bf16[1024,384]{1,0:T(8,128)(2,1)S(1)}, bf16[1024,384]{1,0:T(8,128)(2,1)}, u32[]{:S(2)}) %copy-start.2) | copy-done | bytes 786456
  42.7 1.7 %cross_lags.1 = bf16[256,384]{1,0:T(8,128)(2,1)S(1)} custom-call(f32[32,1024]{1,0:T(8,128)S(1)} %get-tuple-element.8.white_ref, bf16[1024,128]{1,0:T(8,128)(2,1)S(1)} %bitcast.15, f32[128,128]{1,0:T(8,128)S(1)} %get-tuple-element.9.masks_ref, bf16[1024,1024]{1,0:T(8,128)(2,1)S(1)} %copy-done.1, bf16[1024,384]{1,0:T(8,128)(2,1)S(1)} %copy-done.2), custom_call_target="tpu_custom_call" | custom-call | tf_op jit(solution)/shard_map/cross_lags/pallas_call | solution.py:207
  44.4 21.7 %all_to_all.15 = bf16[16,16,384]{2,1,0:T(8,128)(2,1)S(1)} all-to-all(bf16[16,16,384]{2,1,0:T(8,128)(2,1)S(1)} %bitcast.16), channel_id=1, replica_groups=mesh['day'=16,'sta'=32] {'day'}, dimensions={0} | all-to-all | bytes 393216 | tf_op jit(solution)/shard_map/all_to_all | solution.py:217
  66.0 0.7 %sum_parts.1 = f32[8,2,257]{2,1,0:T(2,128)} custom-call(bf16[256,384]{1,0:T(8,128)(2,1)S(1)} %bitcast.17, f32[16,128]{1,0:T(8,128)S(1)} %get-tuple-element.10.scale_ref), custom_call_target="tpu_custom_call" | custom-call | tf_op jit(solution)/shard_map/sum_parts/pallas_call | solution.py:218
  (2 shorter events, 0.0 us)
Async XLA Ops:
  0.0 19.0 %all-to-all-start = ((bf16[32,8,128]{2,1,0:T(8,128)(2,1)}), bf16[32,8,128]{2,1,0:T(8,128)(2,1)S(1)}, u32[]{:S(2)}, u32[]{:S(2)}) async-start(bf16[32,8,128]{2,1,0:T(8,128)(2,1)} %bitcast.18), calls=%async_computation | async-start | bytes 131072 | tf_op jit(solution)/shard_map/all_to_all | solution.py:176
  19.7 19.8 %all-to-all-start.1 = ((bf16[16,4,8,128]{3,2,1,0:T(8,128)(2,1)}), bf16[16,4,8,128]{3,2,1,0:T(8,128)(2,1)S(1)}, u32[]{:S(2)}, u32[]{:S(2)}) async-start(bf16[16,4,8,128]{3,2,1,0:T(8,128)(2,1)} %broadcast_in_dim.2), calls=%async_computation.1 | async-start | bytes 262144 | tf_op jit(solution)/shard_map/all_to_all | solution.py:201
  28.2 1.6 %copy-start = (bf16[1024,1024]{1,0:T(8,128)(2,1)S(1)}, bf16[1024,1024]{1,0:T(8,128)(2,1)}, u32[]{:S(2)}) copy-start(bf16[1024,1024]{1,0:T(8,128)(2,1)} %constant.17.clone.forward_ref) | copy-start | bytes 6291460
  29.8 0.8 %copy-start.3 = (bf16[4,8,1024]{2,1,0:T(8,128)(2,1)S(1)}, bf16[4,8,1024]{2,1,0:T(8,128)(2,1)}, u32[]{:S(2)}) copy-start(bf16[4,8,1024]{2,1,0:T(8,128)(2,1)} %param.5) | copy-start | bytes 196612
  30.6 0.8 %copy-start.4 = (s32[64,256]{1,0:T(8,128)S(1)}, s32[64,256]{1,0:T(8,128)}, u32[]{:S(2)}) copy-start(s32[64,256]{1,0:T(8,128)} %mask_ref.1) | copy-start | bytes 196612
  31.5 0.7 copy-start.5
  32.1 9.4 %copy-start.1 = (bf16[1024,1024]{1,0:T(8,128)(2,1)S(1)}, bf16[1024,1024]{1,0:T(8,128)(2,1)}, u32[]{:S(2)}) copy-start(bf16[1024,1024]{1,0:T(8,128)(2,1)} %constant.17.clone.forward_ref) | copy-start | bytes 6291460
  41.5 1.1 %copy-start.2 = (bf16[1024,384]{1,0:T(8,128)(2,1)S(1)}, bf16[1024,384]{1,0:T(8,128)(2,1)}, u32[]{:S(2)}) copy-start(bf16[1024,384]{1,0:T(8,128)(2,1)} %constant.18.clone.lag_hbm) | copy-start | bytes 2359300

commit v3 on v2

--- a/solution.py
+++ b/solution.py
@@ -101,6 +101,12 @@
     scale_ref[...] = jnp.broadcast_to(1.0 / jnp.sqrt(jnp.maximum(counts, 1.0)), scale_ref.shape)
 
 
+def pick_kernel(owners_ref, tiles_ref, out_ref):
+    picked = jnp.concatenate([tiles_ref[owners_ref[which]] for which in range(OWNERS)], axis=0)
+    for copy in range(out_ref.shape[0]):
+        out_ref[copy] = picked
+
+
 def cross_kernel(
     white_ref, tiles_ref, masks_ref, forward_ref, lag_hbm, out_ref, src_re, src_im, lag_ref, sem
 ):
@@ -193,21 +199,24 @@
         name="prepare",
     )(place, owners, record.reshape(w_dev * sta_dev, samples), alive_mask, forward)
 
-    chosen = jnp.concatenate(
-        [lax.dynamic_slice_in_dim(everyone, owners[which], 1, 0) for which in range(OWNERS)], axis=0
-    )
+    everyone, white, masks, scale = lax.optimization_barrier((everyone, white, masks, scale))
+    copies = pl.pallas_call(
+        pick_kernel,
+        out_shape=jax.ShapeDtypeStruct((sta_count // 2, sources, tiles.shape[2]), record.dtype),
+        in_specs=[in_smem(), in_vmem()],
+        out_specs=in_vmem(),
+        compiler_params=pltpu.CompilerParams(vmem_limit_bytes=8 * 2**20),
+        name="pick_owners",
+    )(owners, everyone)
     cores = [[2 * chip + core for chip in range(sta_count // 2)] for core in range(2)]
     pairs = [[2 * chip, 2 * chip + 1] for chip in range(sta_count // 2)]
-    half = lax.all_to_all(
-        jnp.broadcast_to(chosen[None], (sta_count // 2,) + chosen.shape),
-        "sta", 0, 0, axis_index_groups=cores,
-    )
+    half = lax.all_to_all(copies, "sta", 0, 0, axis_index_groups=cores)
     gathered = lax.all_gather(half, "sta", axis_index_groups=pairs)
 
     pieces = pl.pallas_call(
         cross_kernel,
         out_shape=jax.ShapeDtypeStruct((sources * sta_dev, LANES), jnp.bfloat16),
-        in_specs=[in_vmem()] * 4 + [pl.BlockSpec(memory_space=pl.ANY)],
+        in_specs=[in_vmem()] * 4 + [pl.BlockSpec(memory_space=pltpu.HBM)],
         out_specs=in_vmem(),
         scratch_shapes=[pltpu.VMEM((w_dev * sources, half_len), jnp.float32)] * 2
         + [pltpu.VMEM((samples, LANES), jnp.bfloat16), pltpu.SemaphoreType.DMA],

time: 67.3 us -> 62 us (0.921)
  blocking collectives: 23.7 us -> 39.5 us
  starting transfers between devices: 17.4 us -> 9.18 us
  between operations: 7.47 us -> 0.05 us
  local copies, waits for them, and re-layouts: 7.16 us -> 3.93 us
  waiting for transfers between devices: 7.47 us -> 4.88 us
    all_to_all x0 -> x1, blocking collectives: none -> 15.9 us  [on_device(): half = lax.all_to_all(copies, 'sta', 0, 0, axis_index_groups=cores)]
    all_to_all x1 -> x0, starting transfers between devices: 8.38 us -> none  [on_device(): lax.all_to_all(jnp.broadcast_to(chosen[None], (sta_count // 2,) + chosen....]
    all_to_all x1 -> x0, waiting for transfers between devices: 6.32 us -> none  [on_device(): lax.all_to_all(jnp.broadcast_to(chosen[None], (sta_count // 2,) + chosen....]
    all_to_all x1, waiting for transfers between devices: 1.14 us -> 4.88 us  [on_device(): everyone = lax.all_to_all(tiles, 'sta', 0, 0)]
    slice x1 -> x0, local copies, waits for them, and re-layouts: 1.42 us -> none  [on_device(): owners[which]]
    unnamed x12 -> x14, local copies, waits for them, and re-layouts: 5.06 us -> 3.93 us
  transfers between devices with their start and end apart: 2 -> 1, of which waited for: 2 -> 1; matrix products, arithmetic and copies ran while one was open for 2% -> 0% of each run, Pallas kernels for 2% -> 2%
where the time goes in v3:
time: 62 us; the launch traced here: 61.7 us
  blocking collectives  39.5 us (64%)
  starting transfers between devices  9.18 us (15%)
  waiting for transfers between devices  4.88 us (8%)
  Pallas kernels  4.02 us (6%)
  local copies, waits for them, and re-layouts  3.93 us (6%)
    all_to_all x1, blocking collectives, on_device(): parts = lax.all_to_all(pieces.reshape(day_count, rows, LANES), 'day', 0, 0)  21.7 us
    all_to_all x1, blocking collectives, on_device(): half = lax.all_to_all(copies, 'sta', 0, 0, axis_index_groups=cores)  15.9 us
    all_to_all x1, starting transfers between devices, on_device(): everyone = lax.all_to_all(tiles, 'sta', 0, 0)  9.18 us
    all_to_all x1, waiting for transfers between devices, on_device(): everyone = lax.all_to_all(tiles, 'sta', 0, 0)  4.88 us
    unnamed x14, local copies, waits for them, and re-layouts  3.93 us
    all_gather x1, blocking collectives, on_device(): gathered = lax.all_gather(half, 'sta', axis_index_groups=pairs)  1.98 us
    pallas_call x1, Pallas kernels, on_device(): pl.pallas_call(cross_kernel, out_shape=jax.ShapeDtypeStruct((sources * st...  1.69 us
  transfers between devices with their start and end apart: 1, of which 1 were waited for; matrix products, arithmetic and copies ran while one was open for 0% of the time, Pallas kernels for 2%

profile of v3, /device:TPU:2, one launch (start us, length us, event | category | flops | bytes accessed | tf_op | source)
XLA Modules:
  0.0 61.7 jit_solution(6781397815163944952)
XLA Ops:
  0.0 0.0 copy-start.6
  0.0 9.2 %all-to-all-start = ((bf16[32,8,128]{2,1,0:T(8,128)(2,1)}), bf16[32,8,128]{2,1,0:T(8,128)(2,1)S(1)}, u32[]{:S(2)}, u32[]{:S(2)}) async-start(bf16[32,8,128]{2,1,0:T(8,128)(2,1)} %bitcast.14), calls=%async_computation | async-start | bytes 131072 | tf_op jit(solution)/shard_map/all_to_all | solution.py:182
  9.2 0.1 pad_add_fusion.place_ref
  9.3 0.0 copy-start
  9.3 1.6 %copy-done = bf16[1024,1024]{1,0:T(8,128)(2,1)S(1)} copy-done((bf16[1024,1024]{1,0:T(8,128)(2,1)S(1)}, bf16[1024,1024]{1,0:T(8,128)(2,1)}, u32[]{:S(2)}) %copy-start) | copy-done | bytes 2097176
  10.9 0.0 copy-start.3
  10.9 0.8 %copy-done.3 = bf16[4,8,1024]{2,1,0:T(8,128)(2,1)S(1)} copy-done((bf16[4,8,1024]{2,1,0:T(8,128)(2,1)S(1)}, bf16[4,8,1024]{2,1,0:T(8,128)(2,1)}, u32[]{:S(2)}) %copy-start.3) | copy-done | bytes 65560
  11.7 0.0 copy-start.4
  11.7 0.8 %copy-done.4 = s32[64,256]{1,0:T(8,128)S(1)} copy-done((s32[64,256]{1,0:T(8,128)S(1)}, s32[64,256]{1,0:T(8,128)}, u32[]{:S(2)}) %copy-start.4) | copy-done | bytes 65560
  12.5 0.0 copy-start.5
  12.5 0.7 %copy-done.5 = s32[4]{0:T(128)S(1)} copy-done((s32[4]{0:T(128)S(1)}, s32[4]{0:T(128)}, u32[]{:S(2)}) %copy-start.5) | copy-done | bytes 40
  13.2 0.0 copy-start.1
  13.2 0.0 copy-start.2
  13.2 1.1 %prepare.1 = (f32[32,1024]{1,0:T(8,128)S(1)}, f32[128,128]{1,0:T(8,128)S(1)}, f32[16,128]{1,0:T(8,128)S(1)}) custom-call(s32[2]{0:T(128)S(1)} %pad_add_fusion.place_ref, s32[4]{0:T(128)S(1)} %copy-done.5, bf16[32,1024]{1,0:T(8,128)(2,1)S(1)} %bitcast.15, s32[64,256]{1,0:T(8,128)S(1)} %copy-done.4, bf16[1024,1024]{1,0:T(8,128)(2,1)S(1)} %copy-done), custom_call_target="tpu_custom_call" | custom-call | flops 67108864 | bytes 2097152 | tf_op jit(solution)/shard_map/prepare/pallas_call | solution.py:184
  14.3 4.9 %all-to-all-done.tiles_ref = bf16[32,8,128]{2,1,0:T(8,128)(2,1)S(1)} async-done(((bf16[32,8,128]{2,1,0:T(8,128)(2,1)}), bf16[32,8,128]{2,1,0:T(8,128)(2,1)S(1)}, u32[]{:S(2)}, u32[]{:S(2)}) %all-to-all-start) | async-done | bytes 65568 | tf_op jit(solution)/shard_map/all_to_all | solution.py:182
  19.2 0.0 copy-done.6
  19.2 0.6 pick_owners.1
  19.8 15.9 %all_to_all.15 = bf16[16,32,128]{2,1,0:T(8,128)(2,1)S(1)} all-to-all(bf16[16,32,128]{2,1,0:T(8,128)(2,1)S(1)} %pick_owners.1), channel_id=1, replica_groups={{0,2,4,6,8,10,12,14,16,18,20,22,24,26,28,30},{1,3,5,7,9,11,13,15,17,19,..., dimensions={0} | all-to-all | bytes 262144 | tf_op jit(solution)/shard_map/all_to_all | solution.py:213
  35.6 2.0 %all-gather = bf16[32,32,128]{2,1,0:T(8,128)(2,1)S(1)} all-gather(bf16[16,32,128]{2,1,0:T(8,128)(2,1)S(1)} %all_to_all.15), channel_id=2, replica_groups={{0,1},{2,3},{4,5},{6,7},{8,9},{10,11},{12,13},{14,15},{16,17},{18,19},{..., dimensions={0}, use_global_device_ids=true | all-gather | bytes 393216 | tf_op jit(solution)/shard_map/all_gather | solution.py:214
  37.6 0.0 copy-done.1
  37.6 0.0 copy-done.2
  37.6 1.7 %cross_lags.1 = bf16[256,384]{1,0:T(8,128)(2,1)S(1)} custom-call(f32[32,1024]{1,0:T(8,128)S(1)} %get-tuple-element.15.white_ref, bf16[1024,128]{1,0:T(8,128)(2,1)S(1)} %bitcast.11, f32[128,128]{1,0:T(8,128)S(1)} %get-tuple-element.17.masks_ref, bf16[1024,1024]{1,0:T(8,128)(2,1)S(1)} %copy-done.1, bf16[1024,384]{1,0:T(8,128)(2,1)S(1)} %copy-done.2), custom_call_target="tpu_custom_call" | custom-call | tf_op jit(solution)/shard_map/cross_lags/pallas_call | solution.py:216
  39.3 21.7 %all_to_all.16 = bf16[16,16,384]{2,1,0:T(8,128)(2,1)S(1)} all-to-all(bf16[16,16,384]{2,1,0:T(8,128)(2,1)S(1)} %bitcast.12), channel_id=1, replica_groups=mesh['day'=16,'sta'=32] {'day'}, dimensions={0} | all-to-all | bytes 393216 | tf_op jit(solution)/shard_map/all_to_all | solution.py:226
  61.0 0.7 %sum_parts.1 = f32[8,2,257]{2,1,0:T(2,128)} custom-call(bf16[256,384]{1,0:T(8,128)(2,1)S(1)} %bitcast.13, f32[16,128]{1,0:T(8,128)S(1)} %get-tuple-element.18.scale_ref), custom_call_target="tpu_custom_call" | custom-call | tf_op jit(solution)/shard_map/sum_parts/pallas_call | solution.py:227
Async XLA Ops:
  0.0 19.2 %copy-start.6 = (s32[4]{0:T(128)S(1)}, s32[4]{0:T(128)}, u32[]{:S(2)}) copy-start(s32[4]{0:T(128)} %owners_ref.3) | copy-start | bytes 52
  0.0 19.2 %all-to-all-start = ((bf16[32,8,128]{2,1,0:T(8,128)(2,1)}), bf16[32,8,128]{2,1,0:T(8,128)(2,1)S(1)}, u32[]{:S(2)}, u32[]{:S(2)}) async-start(bf16[32,8,128]{2,1,0:T(8,128)(2,1)} %bitcast.14), calls=%async_computation | async-start | bytes 131072 | tf_op jit(solution)/shard_map/all_to_all | solution.py:182
  9.3 1.6 %copy-start = (bf16[1024,1024]{1,0:T(8,128)(2,1)S(1)}, bf16[1024,1024]{1,0:T(8,128)(2,1)}, u32[]{:S(2)}) copy-start(bf16[1024,1024]{1,0:T(8,128)(2,1)} %constant.13.clone.forward_ref) | copy-start | bytes 6291460
  10.9 0.8 %copy-start.3 = (bf16[4,8,1024]{2,1,0:T(8,128)(2,1)S(1)}, bf16[4,8,1024]{2,1,0:T(8,128)(2,1)}, u32[]{:S(2)}) copy-start(bf16[4,8,1024]{2,1,0:T(8,128)(2,1)} %param.5) | copy-start | bytes 196612
  11.7 0.8 %copy-start.4 = (s32[64,256]{1,0:T(8,128)S(1)}, s32[64,256]{1,0:T(8,128)}, u32[]{:S(2)}) copy-start(s32[64,256]{1,0:T(8,128)} %mask_ref.1) | copy-start | bytes 196612
  12.5 0.7 %copy-start.5 = (s32[4]{0:T(128)S(1)}, s32[4]{0:T(128)}, u32[]{:S(2)}) copy-start(s32[4]{0:T(128)} %owners_ref.3) | copy-start | bytes 52
  13.2 24.4 %copy-start.1 = (bf16[1024,1024]{1,0:T(8,128)(2,1)S(1)}, bf16[1024,1024]{1,0:T(8,128)(2,1)}, u32[]{:S(2)}) copy-start(bf16[1024,1024]{1,0:T(8,128)(2,1)} %constant.13.clone.forward_ref) | copy-start | bytes 6291460
  13.2 24.4 %copy-start.2 = (bf16[1024,384]{1,0:T(8,128)(2,1)S(1)}, bf16[1024,384]{1,0:T(8,128)(2,1)}, u32[]{:S(2)}) copy-start(bf16[1024,384]{1,0:T(8,128)(2,1)} %constant.14.clone.lag_hbm) | copy-start | bytes 2359300

commit v4 on v3

--- a/solution.py
+++ b/solution.py
@@ -12,6 +12,7 @@
 OWNERS = 4
 LANES = 384
 SHARE = 4
+SOURCES = 32
 
 
 def forward_table(samples, half_len):
@@ -61,14 +62,12 @@
     )
 
 
-def prepare_kernel(
-    place_ref, owners_ref, own_ref, mask_ref, forward_ref, white_ref, masks_ref, scale_ref
-):
+def mask_kernel(place_ref, owners_ref, mask_ref, masks_ref, scale_ref):
     day_pos, sta_pos = place_ref[0], place_ref[1]
-    sources = masks_ref.shape[0] // SHARE
-    width = own_ref.shape[0] // SHARE
     stations = mask_ref.shape[1]
     rows = scale_ref.shape[0]
+    sources = SOURCES
+    width = sources // OWNERS
     src_dev = rows // width
     first_window = day_pos * SHARE
     row = lax.broadcasted_iota(jnp.int32, (sources + 2 * rows, stations), 0)
@@ -88,13 +87,10 @@
         jnp.sum(jnp.where(window == first_window + w, alive, 0.0), axis=1, keepdims=True)
         for w in range(SHARE)
     ]
-    for w in range(SHARE):
-        masks_ref[w * sources : (w + 1) * sources, :] = jnp.broadcast_to(
-            now[w][:sources], (sources, masks_ref.shape[1])
-        )
-    own_masks = jnp.concatenate([m[sources : sources + width] for m in now], axis=0)
-    real_part, imag_part = whiten(own_ref[...], forward_ref, own_masks)
-    white_ref[...] = jnp.concatenate([real_part, imag_part], axis=1)
+    column = jnp.concatenate(
+        [m[:sources] for m in now] + [m[sources : sources + width] for m in now], axis=0
+    )
+    masks_ref[...] = jnp.broadcast_to(column, masks_ref.shape)
     counts = jnp.sum(
         alive[sources : sources + rows] * alive[sources + rows :], axis=1, keepdims=True
     )
@@ -108,37 +104,41 @@
 
 
 def cross_kernel(
-    white_ref, tiles_ref, masks_ref, forward_ref, lag_hbm, out_ref, src_re, src_im, lag_ref, sem
+    own_ref, tiles_ref, masks_ref, forward_ref, lag_ref, out_ref, white_re, white_im
 ):
-    fetch = pltpu.make_async_copy(lag_hbm, lag_ref, sem)
-    fetch.start()
-    sources = masks_ref.shape[0] // SHARE
-    width = white_ref.shape[0] // SHARE
-    half_len = src_re.shape[1]
+    width = own_ref.shape[0] // SHARE
+    sources = masks_ref.shape[0] // SHARE - width
+    half_len = white_re.shape[1]
     tiles = tiles_ref.shape[0] // sources
     wide = tiles // SHARE
     rows = []
     for w in range(SHARE):
-        at = [(t % 2) * (tiles // 2) + t // 2 for t in range(w * wide, (w + 1) * wide)]
         rows.append(
-            jnp.concatenate([tiles_ref[a * sources : (a + 1) * sources, :] for a in at], axis=1)
+            jnp.concatenate(
+                [
+                    tiles_ref[t * sources : (t + 1) * sources, :]
+                    for t in range(w * wide, (w + 1) * wide)
+                ],
+                axis=1,
+            )
         )
-    src_re[...], src_im[...] = whiten(
+    rows.append(own_ref[...])
+    white_re[...], white_im[...] = whiten(
         jnp.concatenate(rows, axis=0), forward_ref, masks_ref[:, 0:1]
     )
+    first_own = SHARE * sources
     crossed = []
     for source in range(sources):
         real_sum = jnp.zeros((width, half_len), jnp.float32)
         imag_sum = jnp.zeros((width, half_len), jnp.float32)
         for w in range(SHARE):
             at = w * sources + source
-            re, im = src_re[at : at + 1, :], src_im[at : at + 1, :]
-            mine_re = white_ref[w * width : (w + 1) * width, :half_len]
-            mine_im = white_ref[w * width : (w + 1) * width, half_len:]
+            re, im = white_re[at : at + 1, :], white_im[at : at + 1, :]
+            mine = slice(first_own + w * width, first_own + (w + 1) * width)
+            mine_re, mine_im = white_re[mine, :], white_im[mine, :]
             real_sum = real_sum + (mine_re * re + mine_im * im)
             imag_sum = imag_sum + (mine_im * re - mine_re * im)
         crossed.append(jnp.concatenate([real_sum, imag_sum], axis=1))
-    fetch.wait()
     for first in range(0, sources, 16):
         block = jnp.concatenate(crossed[first : first + 16], axis=0).astype(jnp.bfloat16)
         out_ref[first * width : (first + 16) * width, :] = jnp.dot(
@@ -181,48 +181,46 @@
     tiles = tiles.transpose(0, 2, 1, 3).reshape(sta_count, sta_dev, -1)
     everyone = lax.all_to_all(tiles, "sta", 0, 0)
 
-    white, masks, scale = pl.pallas_call(
-        prepare_kernel,
+    masks, scale = pl.pallas_call(
+        mask_kernel,
         out_shape=[
-            jax.ShapeDtypeStruct((w_dev * sta_dev, samples), jnp.float32),
-            jax.ShapeDtypeStruct((w_dev * sources, 128), jnp.float32),
+            jax.ShapeDtypeStruct((w_dev * (sources + sta_dev), 128), jnp.float32),
             jax.ShapeDtypeStruct((rows, 128), jnp.float32),
         ],
-        in_specs=[in_smem(), in_smem()] + [in_vmem()] * 3,
-        out_specs=[in_vmem()] * 3,
+        in_specs=[in_smem(), in_smem(), in_vmem()],
+        out_specs=[in_vmem()] * 2,
         compiler_params=pltpu.CompilerParams(vmem_limit_bytes=16 * 2**20),
         cost_estimate=pl.CostEstimate(
-            flops=2 * w_dev * sta_dev * samples * samples,
-            bytes_accessed=2 * samples * samples,
-            transcendentals=w_dev * sta_dev * samples,
+            flops=2000000000, bytes_accessed=2097152, transcendentals=0
         ),
-        name="prepare",
-    )(place, owners, record.reshape(w_dev * sta_dev, samples), alive_mask, forward)
-
-    everyone, white, masks, scale = lax.optimization_barrier((everyone, white, masks, scale))
+        name="masks",
+    )(place, owners, alive_mask)
+    everyone, masks, scale = lax.optimization_barrier((everyone, masks, scale))
     copies = pl.pallas_call(
         pick_kernel,
-        out_shape=jax.ShapeDtypeStruct((sta_count // 2, sources, tiles.shape[2]), record.dtype),
+        out_shape=jax.ShapeDtypeStruct((sta_count, sources, tiles.shape[2]), record.dtype),
         in_specs=[in_smem(), in_vmem()],
         out_specs=in_vmem(),
         compiler_params=pltpu.CompilerParams(vmem_limit_bytes=8 * 2**20),
         name="pick_owners",
     )(owners, everyone)
-    cores = [[2 * chip + core for chip in range(sta_count // 2)] for core in range(2)]
-    pairs = [[2 * chip, 2 * chip + 1] for chip in range(sta_count // 2)]
-    half = lax.all_to_all(copies, "sta", 0, 0, axis_index_groups=cores)
-    gathered = lax.all_gather(half, "sta", axis_index_groups=pairs)
+    gathered = lax.all_to_all(copies, "sta", 0, 0)
 
     pieces = pl.pallas_call(
         cross_kernel,
         out_shape=jax.ShapeDtypeStruct((sources * sta_dev, LANES), jnp.bfloat16),
-        in_specs=[in_vmem()] * 4 + [pl.BlockSpec(memory_space=pltpu.HBM)],
+        in_specs=[in_vmem()] * 5,
         out_specs=in_vmem(),
-        scratch_shapes=[pltpu.VMEM((w_dev * sources, half_len), jnp.float32)] * 2
-        + [pltpu.VMEM((samples, LANES), jnp.bfloat16), pltpu.SemaphoreType.DMA],
+        scratch_shapes=[pltpu.VMEM((w_dev * (sources + sta_dev), half_len), jnp.float32)] * 2,
         compiler_params=pltpu.CompilerParams(vmem_limit_bytes=24 * 2**20),
         name="cross_lags",
-    )(white, gathered.reshape(sta_count * sources, -1), masks, forward, lag_rows)
+    )(
+        record.reshape(w_dev * sta_dev, samples),
+        gathered.reshape(sta_count * sources, -1),
+        masks,
+        forward,
+        lag_rows,
+    )
     parts = lax.all_to_all(pieces.reshape(day_count, rows, LANES), "day", 0, 0)
     return pl.pallas_call(
         final_kernel,

time: 62 us -> 59.9 us (0.966)
  the two profiles are of different devices: /device:TPU:2 before, /device:TPU:8 now
where the time goes in v4:
time: 59.9 us; the launch traced here: 59.7 us
  blocking collectives  37.4 us (62%)
  starting transfers between devices  10.2 us (17%)
  waiting for transfers between devices  6.75 us (11%)
  Pallas kernels  3.7 us (6%)
  local copies, waits for them, and re-layouts  1.51 us (3%)
    all_to_all x1, blocking collectives, on_device(): parts = lax.all_to_all(pieces.reshape(day_count, rows, LANES), 'day', 0, 0)  20.7 us
    all_to_all x1, blocking collectives, on_device(): gathered = lax.all_to_all(copies, 'sta', 0, 0)  16.7 us
    all_to_all x1, starting transfers between devices, on_device(): everyone = lax.all_to_all(tiles, 'sta', 0, 0)  10.2 us
    all_to_all x1, waiting for transfers between devices, on_device(): everyone = lax.all_to_all(tiles, 'sta', 0, 0)  6.75 us
    pallas_call x1, Pallas kernels, on_device(): pl.pallas_call(cross_kernel, out_shape=jax.ShapeDtypeStruct((sources * st...  1.6 us
    unnamed x12, local copies, waits for them, and re-layouts  1.51 us
  transfers between devices with their start and end apart: 1, of which 1 were waited for; matrix products, arithmetic and copies ran while one was open for 0% of the time, Pallas kernels for 1%

profile of v4, /device:TPU:8, one launch (start us, length us, event | category | flops | bytes accessed | tf_op | source)
XLA Modules:
  0.0 59.7 jit_solution(17350918224153233159)
XLA Ops:
  0.0 10.2 %all-to-all-start = ((bf16[32,8,128]{2,1,0:T(8,128)(2,1)}), bf16[32,8,128]{2,1,0:T(8,128)(2,1)S(1)}, u32[]{:S(2)}, u32[]{:S(2)}) async-start(bf16[32,8,128]{2,1,0:T(8,128)(2,1)} %bitcast.14), calls=%async_computation | async-start | bytes 131072 | tf_op jit(solution)/shard_map/all_to_all | solution.py:182
  10.2 0.1 pad_add_fusion.place_ref
  10.3 0.0 copy-start.3
  10.3 0.7 %copy-done.3 = s32[4]{0:T(128)S(1)} copy-done((s32[4]{0:T(128)S(1)}, s32[4]{0:T(128)}, u32[]{:S(2)}) %copy-start.3) | copy-done | bytes 40
  10.9 0.0 copy-start.5
  10.9 0.8 %copy-done.5 = s32[64,256]{1,0:T(8,128)S(1)} copy-done((s32[64,256]{1,0:T(8,128)S(1)}, s32[64,256]{1,0:T(8,128)}, u32[]{:S(2)}) %copy-start.5) | copy-done | bytes 65560
  11.8 0.0 copy-start.4
  11.8 0.0 copy-start
  11.8 0.0 copy-start.1
  11.8 0.0 copy-start.2
  11.8 0.8 %masks.1 = (f32[160,128]{1,0:T(8,128)S(1)}, f32[16,128]{1,0:T(8,128)S(1)}) custom-call(s32[2]{0:T(128)S(1)} %pad_add_fusion.place_ref, s32[4]{0:T(128)S(1)} %copy-done.3, s32[64,256]{1,0:T(8,128)S(1)} %copy-done.5), custom_call_target="tpu_custom_call" | custom-call | flops 2000000000 | bytes 2097152 | tf_op jit(solution)/shard_map/masks/pallas_call | solution.py:184
  12.6 6.8 %all-to-all-done.tiles_ref = bf16[32,8,128]{2,1,0:T(8,128)(2,1)S(1)} async-done(((bf16[32,8,128]{2,1,0:T(8,128)(2,1)}), bf16[32,8,128]{2,1,0:T(8,128)(2,1)S(1)}, u32[]{:S(2)}, u32[]{:S(2)}) %all-to-all-start) | async-done | bytes 65568 | tf_op jit(solution)/shard_map/all_to_all | solution.py:182
  19.4 0.0 copy-done.4
  19.4 0.6 pick_owners.1
  19.9 16.7 %all_to_all.15 = bf16[32,32,128]{2,1,0:T(8,128)(2,1)S(1)} all-to-all(bf16[32,32,128]{2,1,0:T(8,128)(2,1)S(1)} %pick_owners.1), channel_id=1, replica_groups=mesh['day'=16,'sta'=32] {'sta'}, dimensions={0} | all-to-all | bytes 524288 | tf_op jit(solution)/shard_map/all_to_all | solution.py:207
  36.7 0.0 copy-done
  36.7 0.0 copy-done.1
  36.7 0.0 copy-done.2
  36.7 1.6 %cross_lags.1 = bf16[256,384]{1,0:T(8,128)(2,1)S(1)} custom-call(bf16[32,1024]{1,0:T(8,128)(2,1)S(1)} %bitcast.15, bf16[1024,128]{1,0:T(8,128)(2,1)S(1)} %bitcast.11, f32[160,128]{1,0:T(8,128)S(1)} %get-tuple-element.13.masks_ref, bf16[1024,1024]{1,0:T(8,128)(2,1)S(1)} %copy-done, bf16[1024,384]{1,0:T(8,128)(2,1)S(1)} %copy-done.1), custom_call_target="tpu_custom_call" | custom-call | tf_op jit(solution)/shard_map/cross_lags/pallas_call | solution.py:209
  38.3 20.7 %all_to_all.16 = bf16[16,16,384]{2,1,0:T(8,128)(2,1)S(1)} all-to-all(bf16[16,16,384]{2,1,0:T(8,128)(2,1)S(1)} %bitcast.13), channel_id=1, replica_groups=mesh['day'=16,'sta'=32] {'day'}, dimensions={0} | all-to-all | bytes 393216 | tf_op jit(solution)/shard_map/all_to_all | solution.py:224
  59.0 0.7 %sum_parts.1 = f32[8,2,257]{2,1,0:T(2,128)} custom-call(bf16[256,384]{1,0:T(8,128)(2,1)S(1)} %bitcast.12, f32[16,128]{1,0:T(8,128)S(1)} %get-tuple-element.14.scale_ref), custom_call_target="tpu_custom_call" | custom-call | tf_op jit(solution)/shard_map/sum_parts/pallas_call | solution.py:225
Async XLA Ops:
  0.0 19.4 %all-to-all-start = ((bf16[32,8,128]{2,1,0:T(8,128)(2,1)}), bf16[32,8,128]{2,1,0:T(8,128)(2,1)S(1)}, u32[]{:S(2)}, u32[]{:S(2)}) async-start(bf16[32,8,128]{2,1,0:T(8,128)(2,1)} %bitcast.14), calls=%async_computation | async-start | bytes 131072 | tf_op jit(solution)/shard_map/all_to_all | solution.py:182
  10.3 0.7 %copy-start.3 = (s32[4]{0:T(128)S(1)}, s32[4]{0:T(128)}, u32[]{:S(2)}) copy-start(s32[4]{0:T(128)} %owners_ref.3) | copy-start | bytes 52
  10.9 0.8 %copy-start.5 = (s32[64,256]{1,0:T(8,128)S(1)}, s32[64,256]{1,0:T(8,128)}, u32[]{:S(2)}) copy-start(s32[64,256]{1,0:T(8,128)} %mask_ref.1) | copy-start | bytes 196612
  11.8 7.6 %copy-start.4 = (s32[4]{0:T(128)S(1)}, s32[4]{0:T(128)}, u32[]{:S(2)}) copy-start(s32[4]{0:T(128)} %owners_ref.3) | copy-start | bytes 52
  11.8 24.9 %copy-start = (bf16[1024,1024]{1,0:T(8,128)(2,1)S(1)}, bf16[1024,1024]{1,0:T(8,128)(2,1)}, u32[]{:S(2)}) copy-start(bf16[1024,1024]{1,0:T(8,128)(2,1)} %constant.13.clone.forward_ref) | copy-start | bytes 6291460
  11.8 24.9 %copy-start.1 = (bf16[1024,384]{1,0:T(8,128)(2,1)S(1)}, bf16[1024,384]{1,0:T(8,128)(2,1)}, u32[]{:S(2)}) copy-start(bf16[1024,384]{1,0:T(8,128)(2,1)} %constant.14.clone.lag_ref) | copy-start | bytes 2359300
  11.8 24.9 %copy-start.2 = (bf16[4,8,1024]{2,1,0:T(8,128)(2,1)S(1)}, bf16[4,8,1024]{2,1,0:T(8,128)(2,1)}, u32[]{:S(2)}) copy-start(bf16[4,8,1024]{2,1,0:T(8,128)(2,1)} %param.5) | copy-start | bytes 196612

commit v5 on v4

--- a/solution.py
+++ b/solution.py
@@ -10,7 +10,6 @@
 
 MAXLAG = 128
 OWNERS = 4
-LANES = 384
 SHARE = 4
 SOURCES = 32
 
@@ -28,7 +27,8 @@
     phase = (bins * shifts % samples).astype(np.float32) * np.float32(2.0 * math.pi / samples)
     weight = (np.where(bins == half_len, 1.0, 2.0) / math.sqrt(samples)).astype(np.float32)
     table = np.concatenate([weight * np.cos(phase), -weight * np.sin(phase)], axis=0)
-    return np.pad(table, ((0, 0), (0, LANES - table.shape[1]))).astype(jnp.bfloat16)
+    table = table.astype(jnp.bfloat16)
+    return table[:, :-1], np.pad(table[:, -1:].T, ((0, 15), (0, 0)))
 
 
 def owner_columns(owners_ref, source, width):
@@ -65,7 +65,7 @@
 def mask_kernel(place_ref, owners_ref, mask_ref, masks_ref, scale_ref):
     day_pos, sta_pos = place_ref[0], place_ref[1]
     stations = mask_ref.shape[1]
-    rows = scale_ref.shape[0]
+    rows = scale_ref.shape[0] // 2
     sources = SOURCES
     width = sources // OWNERS
     src_dev = rows // width
@@ -94,7 +94,11 @@
     counts = jnp.sum(
         alive[sources : sources + rows] * alive[sources + rows :], axis=1, keepdims=True
     )
-    scale_ref[...] = jnp.broadcast_to(1.0 / jnp.sqrt(jnp.maximum(counts, 1.0)), scale_ref.shape)
+    lanes = scale_ref.shape[1]
+    scale = jnp.broadcast_to(1.0 / jnp.sqrt(jnp.maximum(counts, 1.0)), (rows, lanes))
+    lane = lax.broadcasted_iota(jnp.int32, scale.shape, 1)
+    arrives = lax.rem(day_pos * rows, lanes) + lax.broadcasted_iota(jnp.int32, scale.shape, 0)
+    scale_ref[...] = jnp.concatenate([scale, jnp.where(lane == arrives, scale, 0.0)], axis=0)
 
 
 def pick_kernel(owners_ref, tiles_ref, out_ref):
@@ -104,7 +108,7 @@
 
 
 def cross_kernel(
-    own_ref, tiles_ref, masks_ref, forward_ref, lag_ref, out_ref, white_re, white_im
+    own_ref, tiles_ref, masks_ref, forward_ref, lag_ref, last_ref, out_ref, white_re, white_im
 ):
     width = own_ref.shape[0] // SHARE
     sources = masks_ref.shape[0] // SHARE - width
@@ -139,22 +143,37 @@
             real_sum = real_sum + (mine_re * re + mine_im * im)
             imag_sum = imag_sum + (mine_im * re - mine_re * im)
         crossed.append(jnp.concatenate([real_sum, imag_sum], axis=1))
-    for first in range(0, sources, 16):
-        block = jnp.concatenate(crossed[first : first + 16], axis=0).astype(jnp.bfloat16)
-        out_ref[first * width : (first + 16) * width, :] = jnp.dot(
-            block, lag_ref[...], preferred_element_type=jnp.float32
-        ).astype(out_ref.dtype)
+    lanes = out_ref.shape[2]
+    piece = sources * width // out_ref.shape[0]
+    step = lanes // width
+    for first in range(0, sources, step):
+        block = jnp.concatenate(crossed[first : first + step], axis=0).astype(jnp.bfloat16)
+        lags = jnp.dot(block, lag_ref[...], preferred_element_type=jnp.float32)
+        last = lax.dot_general(
+            last_ref[...], block, (((1,), (1,)), ((), ())), preferred_element_type=jnp.float32
+        )
+        for at in range(0, lanes, piece):
+            out_ref[(first * width + at) // piece] = jnp.concatenate(
+                [lags[at : at + piece, :lanes], lags[at : at + piece, lanes:], last[:8]], axis=0
+            ).astype(out_ref.dtype)
 
 
 def final_kernel(parts_ref, scale_ref, out_ref):
     width, src_dev, lags = out_ref.shape
     rows = width * src_dev
-    total = parts_ref[0:rows, :].astype(jnp.float32)
-    for part in range(1, parts_ref.shape[0] // rows):
-        total = total + parts_ref[part * rows : (part + 1) * rows, :].astype(jnp.float32)
-    total = total * scale_ref[:, 0:1]
+    lanes = parts_ref.shape[2]
+    total = parts_ref[0].astype(jnp.float32)
+    for part in range(1, parts_ref.shape[0]):
+        total = total + parts_ref[part].astype(jnp.float32)
+    scale = scale_ref[:rows]
+    early = total[:rows] * scale
+    late = total[rows : 2 * rows] * scale
+    last = jnp.sum(total[2 * rows : 2 * rows + 1] * scale_ref[rows:], axis=1, keepdims=True)
     for which in range(src_dev):
-        out_ref[:, which, :] = total[which * width : (which + 1) * width, :lags]
+        at = slice(which * width, (which + 1) * width)
+        out_ref[:, which, :lanes] = early[at]
+        out_ref[:, which, lanes : lags - 1] = late[at]
+        out_ref[:, which, lags - 1 :] = last[at]
 
 
 def in_vmem():
@@ -170,7 +189,7 @@
     half_len = samples // 2
     sources = OWNERS * sta_dev
     forward = jnp.asarray(forward_table(samples, half_len))
-    lag_rows = jnp.asarray(lag_table(samples, half_len, MAXLAG))
+    lag_rows, last_row = map(jnp.asarray, lag_table(samples, half_len, MAXLAG))
     day_count, sta_count = lax.axis_size("day"), lax.axis_size("sta")
     day_pos, sta_pos = lax.axis_index("day"), lax.axis_index("sta")
     src_dev = sources // day_count
@@ -185,7 +204,7 @@
         mask_kernel,
         out_shape=[
             jax.ShapeDtypeStruct((w_dev * (sources + sta_dev), 128), jnp.float32),
-            jax.ShapeDtypeStruct((rows, 128), jnp.float32),
+            jax.ShapeDtypeStruct((2 * rows, 128), jnp.float32),
         ],
         in_specs=[in_smem(), in_smem(), in_vmem()],
         out_specs=[in_vmem()] * 2,
@@ -208,8 +227,8 @@
 
     pieces = pl.pallas_call(
         cross_kernel,
-        out_shape=jax.ShapeDtypeStruct((sources * sta_dev, LANES), jnp.bfloat16),
-        in_specs=[in_vmem()] * 5,
+        out_shape=jax.ShapeDtypeStruct((day_count, 2 * rows + 8, 128), jnp.bfloat16),
+        in_specs=[in_vmem()] * 6,
         out_specs=in_vmem(),
         scratch_shapes=[pltpu.VMEM((w_dev * (sources + sta_dev), half_len), jnp.float32)] * 2,
         compiler_params=pltpu.CompilerParams(vmem_limit_bytes=24 * 2**20),
@@ -220,8 +239,9 @@
         masks,
         forward,
         lag_rows,
-    )
-    parts = lax.all_to_all(pieces.reshape(day_count, rows, LANES), "day", 0, 0)
+        last_row,
+    )
+    parts = lax.all_to_all(pieces, "day", 0, 0)
     return pl.pallas_call(
         final_kernel,
         out_shape=jax.ShapeDtypeStruct((sta_dev, src_dev, 2 * MAXLAG + 1), jnp.float32),
@@ -229,7 +249,7 @@
         out_specs=in_vmem(),
         compiler_params=pltpu.CompilerParams(vmem_limit_bytes=16 * 2**20),
         name="sum_parts",
-    )(parts.reshape(day_count * rows, LANES), scale)
+    )(parts, scale)
 
 
 def solution(mesh):

time: 59.9 us -> 59.4 us (level)
    unnamed x12 -> x14, local copies, waits for them, and re-layouts: 1.51 us -> 1.52 us
where the time goes in v5:
time: 59.4 us; the launch traced here: 59.1 us
  blocking collectives  37 us (62%)
  starting transfers between devices  10.2 us (17%)
  waiting for transfers between devices  6.74 us (11%)
  Pallas kernels  3.49 us (6%)
  local copies, waits for them, and re-layouts  1.52 us (3%)
    all_to_all x1, blocking collectives, on_device(): parts = lax.all_to_all(pieces, 'day', 0, 0)  20.3 us
    all_to_all x1, blocking collectives, on_device(): gathered = lax.all_to_all(copies, 'sta', 0, 0)  16.7 us
    all_to_all x1, starting transfers between devices, on_device(): everyone = lax.all_to_all(tiles, 'sta', 0, 0)  10.2 us
    all_to_all x1, waiting for transfers between devices, on_device(): everyone = lax.all_to_all(tiles, 'sta', 0, 0)  6.74 us
    unnamed x14, local copies, waits for them, and re-layouts  1.52 us
    pallas_call x1, Pallas kernels, on_device(): pl.pallas_call(cross_kernel, out_shape=jax.ShapeDtypeStruct((day_count, 2...  1.37 us
  transfers between devices with their start and end apart: 1, of which 1 were waited for; matrix products, arithmetic and copies ran while one was open for 0% of the time, Pallas kernels for 1%

profile of v5, /device:TPU:8, one launch (start us, length us, event | category | flops | bytes accessed | tf_op | source)
XLA Modules:
  0.0 59.1 jit_solution(14528889678363387457)
XLA Ops:
  0.0 10.2 %all-to-all-start = ((bf16[32,8,128]{2,1,0:T(8,128)(2,1)}), bf16[32,8,128]{2,1,0:T(8,128)(2,1)S(1)}, u32[]{:S(2)}, u32[]{:S(2)}) async-start(bf16[32,8,128]{2,1,0:T(8,128)(2,1)} %bitcast.10), calls=%async_computation | async-start | bytes 131072 | tf_op jit(solution)/shard_map/all_to_all | solution.py:201
  10.2 0.1 pad_add_fusion.place_ref
  10.3 0.0 copy-start.4
  10.3 0.7 %copy-done.4 = s32[4]{0:T(128)S(1)} copy-done((s32[4]{0:T(128)S(1)}, s32[4]{0:T(128)}, u32[]{:S(2)}) %copy-start.4) | copy-done | bytes 40
  10.9 0.0 copy-start.6
  10.9 0.8 %copy-done.6 = s32[64,256]{1,0:T(8,128)S(1)} copy-done((s32[64,256]{1,0:T(8,128)S(1)}, s32[64,256]{1,0:T(8,128)}, u32[]{:S(2)}) %copy-start.6) | copy-done | bytes 65560
  11.8 0.0 copy-start.5
  11.8 0.0 copy-start
  11.8 0.0 copy-start.1
  11.8 0.0 copy-start.2
  11.8 0.0 copy-start.3
  11.8 0.8 %masks.1 = (f32[160,128]{1,0:T(8,128)S(1)}, f32[32,128]{1,0:T(8,128)S(1)}) custom-call(s32[2]{0:T(128)S(1)} %pad_add_fusion.place_ref, s32[4]{0:T(128)S(1)} %copy-done.4, s32[64,256]{1,0:T(8,128)S(1)} %copy-done.6), custom_call_target="tpu_custom_call" | custom-call | flops 2000000000 | bytes 2097152 | tf_op jit(solution)/shard_map/masks/pallas_call | solution.py:203
  12.6 6.7 %all-to-all-done.tiles_ref = bf16[32,8,128]{2,1,0:T(8,128)(2,1)S(1)} async-done(((bf16[32,8,128]{2,1,0:T(8,128)(2,1)}), bf16[32,8,128]{2,1,0:T(8,128)(2,1)S(1)}, u32[]{:S(2)}, u32[]{:S(2)}) %all-to-all-start) | async-done | bytes 65568 | tf_op jit(solution)/shard_map/all_to_all | solution.py:201
  19.4 0.0 copy-done.5
  19.4 0.6 pick_owners.1
  19.9 16.7 %all_to_all.15 = bf16[32,32,128]{2,1,0:T(8,128)(2,1)S(1)} all-to-all(bf16[32,32,128]{2,1,0:T(8,128)(2,1)S(1)} %pick_owners.1), channel_id=1, replica_groups=mesh['day'=16,'sta'=32] {'sta'}, dimensions={0} | all-to-all | bytes 524288 | tf_op jit(solution)/shard_map/all_to_all | solution.py:226
  36.7 0.0 copy-done
  36.7 0.0 copy-done.1
  36.7 0.0 copy-done.2
  36.7 0.0 copy-done.3
  36.7 1.4 %cross_lags.1 = bf16[16,40,128]{2,1,0:T(8,128)(2,1)S(1)} custom-call(bf16[32,1024]{1,0:T(8,128)(2,1)S(1)} %bitcast.11, bf16[1024,128]{1,0:T(8,128)(2,1)S(1)} %bitcast.9, f32[160,128]{1,0:T(8,128)S(1)} %get-tuple-element.13.masks_ref, bf16[1024,1024]{1,0:T(8,128)(2,1)S(1)} %copy-done, bf16[1024,256]{1,0:T(8,128)(2,1)S(1)} %copy-done.1, ...), custom_call_target="tpu_custom_call" | custom-call | tf_op jit(solution)/shard_map/cross_lags/pallas_call | solution.py:228
  38.1 20.3 %all_to_all.16.parts_ref = bf16[16,40,128]{2,1,0:T(8,128)(2,1)S(1)} all-to-all(bf16[16,40,128]{2,1,0:T(8,128)(2,1)S(1)} %cross_lags.1), channel_id=1, replica_groups=mesh['day'=16,'sta'=32] {'day'}, dimensions={0} | all-to-all | bytes 327680 | tf_op jit(solution)/shard_map/all_to_all | solution.py:244
  58.4 0.7 %sum_parts.1 = f32[8,2,257]{2,1,0:T(2,128)} custom-call(bf16[16,40,128]{2,1,0:T(8,128)(2,1)S(1)} %all_to_all.16.parts_ref, f32[32,128]{1,0:T(8,128)S(1)} %get-tuple-element.14.scale_ref), custom_call_target="tpu_custom_call" | custom-call | tf_op jit(solution)/shard_map/sum_parts/pallas_call | solution.py:245
Async XLA Ops:
  0.0 19.4 %all-to-all-start = ((bf16[32,8,128]{2,1,0:T(8,128)(2,1)}), bf16[32,8,128]{2,1,0:T(8,128)(2,1)S(1)}, u32[]{:S(2)}, u32[]{:S(2)}) async-start(bf16[32,8,128]{2,1,0:T(8,128)(2,1)} %bitcast.10), calls=%async_computation | async-start | bytes 131072 | tf_op jit(solution)/shard_map/all_to_all | solution.py:201
  10.3 0.7 %copy-start.4 = (s32[4]{0:T(128)S(1)}, s32[4]{0:T(128)}, u32[]{:S(2)}) copy-start(s32[4]{0:T(128)} %owners_ref.3) | copy-start | bytes 52
  10.9 0.8 %copy-start.6 = (s32[64,256]{1,0:T(8,128)S(1)}, s32[64,256]{1,0:T(8,128)}, u32[]{:S(2)}) copy-start(s32[64,256]{1,0:T(8,128)} %mask_ref.1) | copy-start | bytes 196612
  11.8 7.6 %copy-start.5 = (s32[4]{0:T(128)S(1)}, s32[4]{0:T(128)}, u32[]{:S(2)}) copy-start(s32[4]{0:T(128)} %owners_ref.3) | copy-start | bytes 52
  11.8 24.9 %copy-start = (bf16[1024,1024]{1,0:T(8,128)(2,1)S(1)}, bf16[1024,1024]{1,0:T(8,128)(2,1)}, u32[]{:S(2)}) copy-start(bf16[1024,1024]{1,0:T(8,128)(2,1)} %constant.15.clone.forward_ref) | copy-start | bytes 6291460
  11.8 24.9 %copy-start.1 = (bf16[1024,256]{1,0:T(8,128)(2,1)S(1)}, bf16[1024,256]{1,0:T(8,128)(2,1)}, u32[]{:S(2)}) copy-start(bf16[1024,256]{1,0:T(8,128)(2,1)} %constant.16.clone.lag_ref) | copy-start | bytes 1572868
  11.8 24.9 %copy-start.2 = (bf16[4,8,1024]{2,1,0:T(8,128)(2,1)S(1)}, bf16[4,8,1024]{2,1,0:T(8,128)(2,1)}, u32[]{:S(2)}) copy-start(bf16[4,8,1024]{2,1,0:T(8,128)(2,1)} %param.6) | copy-start | bytes 196612
  11.8 24.9 %copy-start.3 = (bf16[16,1024]{1,0:T(8,128)(2,1)S(1)}, bf16[16,1024]{1,0:T(8,128)(2,1)}, u32[]{:S(2)}) copy-start(bf16[16,1024]{1,0:T(8,128)(2,1)} %constant.17.clone.last_ref) | copy-start | bytes 98308

commit v6 on v5

--- a/solution.py
+++ b/solution.py
@@ -12,6 +12,7 @@
 OWNERS = 4
 SHARE = 4
 SOURCES = 32
+GROUP = 8
 
 
 def forward_table(samples, half_len):
@@ -102,7 +103,14 @@
 
 
 def pick_kernel(owners_ref, tiles_ref, out_ref):
-    picked = jnp.concatenate([tiles_ref[owners_ref[which]] for which in range(OWNERS)], axis=0)
+    picked = jnp.concatenate(
+        [
+            tiles_ref[owners_ref[which], part]
+            for part in range(tiles_ref.shape[1])
+            for which in range(OWNERS)
+        ],
+        axis=0,
+    )
     for copy in range(out_ref.shape[0]):
         out_ref[copy] = picked
 
@@ -196,8 +204,9 @@
     rows = src_dev * sta_dev
     place = jnp.stack([day_pos, sta_pos]).astype(jnp.int32)
 
-    tiles = record.reshape(w_dev, sta_dev, sta_count // w_dev, -1)
-    tiles = tiles.transpose(0, 2, 1, 3).reshape(sta_count, sta_dev, -1)
+    blocks = jnp.broadcast_to(record[None], (sta_count // GROUP,) + record.shape)
+    tiles = blocks.reshape(sta_count // GROUP, w_dev, sta_dev, sta_count // w_dev, -1)
+    tiles = tiles.transpose(0, 1, 3, 2, 4).reshape(sta_count, sta_count // GROUP, sta_dev, -1)
     everyone = lax.all_to_all(tiles, "sta", 0, 0)
 
     masks, scale = pl.pallas_call(
@@ -217,13 +226,14 @@
     everyone, masks, scale = lax.optimization_barrier((everyone, masks, scale))
     copies = pl.pallas_call(
         pick_kernel,
-        out_shape=jax.ShapeDtypeStruct((sta_count, sources, tiles.shape[2]), record.dtype),
+        out_shape=jax.ShapeDtypeStruct((GROUP, SOURCES * sta_count // GROUP, tiles.shape[3]), record.dtype),
         in_specs=[in_smem(), in_vmem()],
         out_specs=in_vmem(),
         compiler_params=pltpu.CompilerParams(vmem_limit_bytes=8 * 2**20),
         name="pick_owners",
     )(owners, everyone)
-    gathered = lax.all_to_all(copies, "sta", 0, 0)
+    groups = [list(range(first, first + GROUP)) for first in range(0, sta_count, GROUP)]
+    gathered = lax.all_to_all(copies, "sta", 0, 0, axis_index_groups=groups)
 
     pieces = pl.pallas_call(
         cross_kernel,

time: 59.4 us -> 58.9 us (level)
  blocking collectives: 37 us -> 31.1 us
  waiting for transfers between devices: 6.74 us -> 10.6 us
  local copies, waits for them, and re-layouts: 1.52 us -> 3.11 us
    all_to_all x1, blocking collectives: 16.7 us -> 10.7 us  [on_device(): gathered = lax.all_to_all(copies, 'sta', 0, 0, axis_index_groups=groups)]
    all_to_all x1, waiting for transfers between devices: 6.74 us -> 10.6 us  [on_device(): everyone = lax.all_to_all(tiles, 'sta', 0, 0)]
    broadcast_in_dim x0 -> x1, local copies, waits for them, and re-layouts: none -> 1.59 us  [on_device(): jnp.broadcast_to(record[None], (sta_count // GROUP,) + record.shape)]
where the time goes in v6:
time: 58.9 us; the launch traced here: 58.5 us
  blocking collectives  31.1 us (53%)
  waiting for transfers between devices  10.6 us (18%)
  starting transfers between devices  10.2 us (17%)
  Pallas kernels  3.49 us (6%)
  local copies, waits for them, and re-layouts  3.11 us (5%)
    all_to_all x1, blocking collectives, on_device(): parts = lax.all_to_all(pieces, 'day', 0, 0)  20.4 us
    all_to_all x1, blocking collectives, on_device(): gathered = lax.all_to_all(copies, 'sta', 0, 0, axis_index_groups=groups)  10.7 us
    all_to_all x1, waiting for transfers between devices, on_device(): everyone = lax.all_to_all(tiles, 'sta', 0, 0)  10.6 us
    all_to_all x1, starting transfers between devices, on_device(): everyone = lax.all_to_all(tiles, 'sta', 0, 0)  10.2 us
    broadcast_in_dim x1, local copies, waits for them, and re-layouts, on_device(): jnp.broadcast_to(record[None], (sta_count // GROUP,) + record.shape)  1.59 us
    unnamed x14, local copies, waits for them, and re-layouts  1.52 us
    pallas_call x1, Pallas kernels, on_device(): pl.pallas_call(cross_kernel, out_shape=jax.ShapeDtypeStruct((day_count, 2...  1.37 us
  transfers between devices with their start and end apart: 1, of which 1 were waited for; matrix products, arithmetic and copies ran while one was open for 0% of the time, Pallas kernels for 1%

profile of v6, /device:TPU:8, one launch (start us, length us, event | category | flops | bytes accessed | tf_op | source)
XLA Modules:
  0.0 58.5 jit_solution(2189575372913290811)
XLA Ops:
  0.0 1.6 %broadcast_in_dim.9 = bf16[4,4,8,8,128]{4,2,3,1,0:T(8,128)(2,1)} broadcast(bf16[4,8,8,128]{3,1,2,0:T(8,128)(2,1)} %bitcast.9), dimensions={1,2,3,4} | broadcast | bytes 327680 | tf_op jit(solution)/shard_map/broadcast_in_dim | solution.py:207
  1.6 10.2 %all-to-all-start = ((bf16[32,4,8,128]{3,2,1,0:T(8,128)(2,1)}), bf16[32,4,8,128]{3,2,1,0:T(8,128)(2,1)S(1)}, u32[]{:S(2)}, u32[]{:S(2)}) async-start(bf16[32,4,8,128]{3,2,1,0:T(8,128)(2,1)} %bitcast.3), calls=%async_computation | async-start | bytes 524288 | tf_op jit(solution)/shard_map/all_to_all | solution.py:210
  11.8 0.1 pad_add_fusion.place_ref
  11.8 0.0 copy-start.4
  11.8 0.7 %copy-done.4 = s32[4]{0:T(128)S(1)} copy-done((s32[4]{0:T(128)S(1)}, s32[4]{0:T(128)}, u32[]{:S(2)}) %copy-start.4) | copy-done | bytes 40
  12.5 0.0 copy-start.6
  12.5 0.8 %copy-done.6 = s32[64,256]{1,0:T(8,128)S(1)} copy-done((s32[64,256]{1,0:T(8,128)S(1)}, s32[64,256]{1,0:T(8,128)}, u32[]{:S(2)}) %copy-start.6) | copy-done | bytes 65560
  13.3 0.0 copy-start.5
  13.3 0.0 copy-start
  13.3 0.0 copy-start.1
  13.3 0.0 copy-start.2
  13.4 0.0 copy-start.3
  13.4 0.8 %masks.1 = (f32[160,128]{1,0:T(8,128)S(1)}, f32[32,128]{1,0:T(8,128)S(1)}) custom-call(s32[2]{0:T(128)S(1)} %pad_add_fusion.place_ref, s32[4]{0:T(128)S(1)} %copy-done.4, s32[64,256]{1,0:T(8,128)S(1)} %copy-done.6), custom_call_target="tpu_custom_call" | custom-call | flops 2000000000 | bytes 2097152 | tf_op jit(solution)/shard_map/masks/pallas_call | solution.py:212
  14.2 10.6 %all-to-all-done.tiles_ref = bf16[32,4,8,128]{3,2,1,0:T(8,128)(2,1)S(1)} async-done(((bf16[32,4,8,128]{3,2,1,0:T(8,128)(2,1)}), bf16[32,4,8,128]{3,2,1,0:T(8,128)(2,1)S(1)}, u32[]{:S(2)}, u32[]{:S(2)}) %all-to-all-start) | async-done | bytes 262176 | tf_op jit(solution)/shard_map/all_to_all | solution.py:210
  24.8 0.0 copy-done.5
  24.8 0.6 pick_owners.1
  25.4 10.7 %all_to_all.15 = bf16[8,128,128]{2,1,0:T(8,128)(2,1)S(1)} all-to-all(bf16[8,128,128]{2,1,0:T(8,128)(2,1)S(1)} %pick_owners.1), channel_id=1, replica_groups={{0,1,2,3,4,5,6,7},{8,9,10,11,12,13,14,15},{16,17,18,19,20,21,22,23},{24..., dimensions={0} | all-to-all | bytes 524288 | tf_op jit(solution)/shard_map/all_to_all | solution.py:236
  36.1 0.0 copy-done
  36.1 0.0 copy-done.1
  36.1 0.0 copy-done.2
  36.1 0.0 copy-done.3
  36.1 1.4 %cross_lags.1 = bf16[16,40,128]{2,1,0:T(8,128)(2,1)S(1)} custom-call(bf16[32,1024]{1,0:T(8,128)(2,1)S(1)} %bitcast.10, bf16[1024,128]{1,0:T(8,128)(2,1)S(1)} %bitcast.8, f32[160,128]{1,0:T(8,128)S(1)} %get-tuple-element.13.masks_ref, bf16[1024,1024]{1,0:T(8,128)(2,1)S(1)} %copy-done, bf16[1024,256]{1,0:T(8,128)(2,1)S(1)} %copy-done.1, ...), custom_call_target="tpu_custom_call" | custom-call | tf_op jit(solution)/shard_map/cross_lags/pallas_call | solution.py:238
  37.4 20.4 %all_to_all.16.parts_ref = bf16[16,40,128]{2,1,0:T(8,128)(2,1)S(1)} all-to-all(bf16[16,40,128]{2,1,0:T(8,128)(2,1)S(1)} %cross_lags.1), channel_id=1, replica_groups=mesh['day'=16,'sta'=32] {'day'}, dimensions={0} | all-to-all | bytes 327680 | tf_op jit(solution)/shard_map/all_to_all | solution.py:254
  57.8 0.7 %sum_parts.1 = f32[8,2,257]{2,1,0:T(2,128)} custom-call(bf16[16,40,128]{2,1,0:T(8,128)(2,1)S(1)} %all_to_all.16.parts_ref, f32[32,128]{1,0:T(8,128)S(1)} %get-tuple-element.14.scale_ref), custom_call_target="tpu_custom_call" | custom-call | tf_op jit(solution)/shard_map/sum_parts/pallas_call | solution.py:255
Async XLA Ops:
  1.6 23.2 %all-to-all-start = ((bf16[32,4,8,128]{3,2,1,0:T(8,128)(2,1)}), bf16[32,4,8,128]{3,2,1,0:T(8,128)(2,1)S(1)}, u32[]{:S(2)}, u32[]{:S(2)}) async-start(bf16[32,4,8,128]{3,2,1,0:T(8,128)(2,1)} %bitcast.3), calls=%async_computation | async-start | bytes 524288 | tf_op jit(solution)/shard_map/all_to_all | solution.py:210
  11.8 0.7 %copy-start.4 = (s32[4]{0:T(128)S(1)}, s32[4]{0:T(128)}, u32[]{:S(2)}) copy-start(s32[4]{0:T(128)} %owners_ref.3) | copy-start | bytes 52
  12.5 0.8 %copy-start.6 = (s32[64,256]{1,0:T(8,128)S(1)}, s32[64,256]{1,0:T(8,128)}, u32[]{:S(2)}) copy-start(s32[64,256]{1,0:T(8,128)} %mask_ref.1) | copy-start | bytes 196612
  13.3 11.4 %copy-start.5 = (s32[4]{0:T(128)S(1)}, s32[4]{0:T(128)}, u32[]{:S(2)}) copy-start(s32[4]{0:T(128)} %owners_ref.3) | copy-start | bytes 52
  13.3 22.7 %copy-start = (bf16[1024,1024]{1,0:T(8,128)(2,1)S(1)}, bf16[1024,1024]{1,0:T(8,128)(2,1)}, u32[]{:S(2)}) copy-start(bf16[1024,1024]{1,0:T(8,128)(2,1)} %constant.15.clone.forward_ref) | copy-start | bytes 6291460
  13.3 22.7 %copy-start.1 = (bf16[1024,256]{1,0:T(8,128)(2,1)S(1)}, bf16[1024,256]{1,0:T(8,128)(2,1)}, u32[]{:S(2)}) copy-start(bf16[1024,256]{1,0:T(8,128)(2,1)} %constant.16.clone.lag_ref) | copy-start | bytes 1572868
  13.3 22.7 %copy-start.2 = (bf16[4,8,1024]{2,1,0:T(8,128)(2,1)S(1)}, bf16[4,8,1024]{2,1,0:T(8,128)(2,1)}, u32[]{:S(2)}) copy-start(bf16[4,8,1024]{2,1,0:T(8,128)(2,1)} %param.6) | copy-start | bytes 196612
  13.4 22.7 %copy-start.3 = (bf16[16,1024]{1,0:T(8,128)(2,1)S(1)}, bf16[16,1024]{1,0:T(8,128)(2,1)}, u32[]{:S(2)}) copy-start(bf16[16,1024]{1,0:T(8,128)(2,1)} %constant.17.clone.last_ref) | copy-start | bytes 98308

commit v7 on v6

--- a/solution.py
+++ b/solution.py
@@ -63,10 +63,9 @@
     )
 
 
-def mask_kernel(place_ref, owners_ref, mask_ref, masks_ref, scale_ref):
+def mask_columns(place_ref, owners_ref, mask_ref, rows, lanes):
     day_pos, sta_pos = place_ref[0], place_ref[1]
     stations = mask_ref.shape[1]
-    rows = scale_ref.shape[0] // 2
     sources = SOURCES
     width = sources // OWNERS
     src_dev = rows // width
@@ -91,18 +90,27 @@
     column = jnp.concatenate(
         [m[:sources] for m in now] + [m[sources : sources + width] for m in now], axis=0
     )
-    masks_ref[...] = jnp.broadcast_to(column, masks_ref.shape)
     counts = jnp.sum(
         alive[sources : sources + rows] * alive[sources + rows :], axis=1, keepdims=True
     )
-    lanes = scale_ref.shape[1]
     scale = jnp.broadcast_to(1.0 / jnp.sqrt(jnp.maximum(counts, 1.0)), (rows, lanes))
     lane = lax.broadcasted_iota(jnp.int32, scale.shape, 1)
     arrives = lax.rem(day_pos * rows, lanes) + lax.broadcasted_iota(jnp.int32, scale.shape, 0)
-    scale_ref[...] = jnp.concatenate([scale, jnp.where(lane == arrives, scale, 0.0)], axis=0)
-
-
-def pick_kernel(owners_ref, tiles_ref, out_ref):
+    return column, jnp.concatenate([scale, jnp.where(lane == arrives, scale, 0.0)], axis=0)
+
+
+def spread_kernel(record_ref, out_ref):
+    for copy in range(out_ref.shape[0]):
+        out_ref[copy] = record_ref[...]
+
+
+def pick_kernel(
+    place_ref, owners_ref, tiles_ref, mask_ref, out_ref, masks_ref, scale_ref
+):
+    column, scale_ref[...] = mask_columns(
+        place_ref, owners_ref, mask_ref, scale_ref.shape[0] // 2, scale_ref.shape[1]
+    )
+    masks_ref[...] = jnp.broadcast_to(column, masks_ref.shape)
     picked = jnp.concatenate(
         [
             tiles_ref[owners_ref[which], part]
@@ -204,34 +212,39 @@
     rows = src_dev * sta_dev
     place = jnp.stack([day_pos, sta_pos]).astype(jnp.int32)
 
-    blocks = jnp.broadcast_to(record[None], (sta_count // GROUP,) + record.shape)
+    record, place = lax.optimization_barrier((record, place))
+    blocks = pl.pallas_call(
+        spread_kernel,
+        out_shape=jax.ShapeDtypeStruct((sta_count // GROUP,) + record.shape, record.dtype),
+        in_specs=[in_vmem()],
+        out_specs=in_vmem(),
+        compiler_params=pltpu.CompilerParams(vmem_limit_bytes=8 * 2**20),
+        cost_estimate=pl.CostEstimate(
+            flops=4 * 10**9, bytes_accessed=2**19, transcendentals=0
+        ),
+        name="spread",
+    )(record)
     tiles = blocks.reshape(sta_count // GROUP, w_dev, sta_dev, sta_count // w_dev, -1)
     tiles = tiles.transpose(0, 1, 3, 2, 4).reshape(sta_count, sta_count // GROUP, sta_dev, -1)
     everyone = lax.all_to_all(tiles, "sta", 0, 0)
 
-    masks, scale = pl.pallas_call(
-        mask_kernel,
+    copies, masks, scale = pl.pallas_call(
+        pick_kernel,
         out_shape=[
+            jax.ShapeDtypeStruct(
+                (GROUP, SOURCES * sta_count // GROUP, tiles.shape[3]), record.dtype
+            ),
             jax.ShapeDtypeStruct((w_dev * (sources + sta_dev), 128), jnp.float32),
             jax.ShapeDtypeStruct((2 * rows, 128), jnp.float32),
         ],
-        in_specs=[in_smem(), in_smem(), in_vmem()],
-        out_specs=[in_vmem()] * 2,
-        compiler_params=pltpu.CompilerParams(vmem_limit_bytes=16 * 2**20),
+        in_specs=[in_smem(), in_smem()] + [in_vmem()] * 2,
+        out_specs=[in_vmem()] * 3,
+        compiler_params=pltpu.CompilerParams(vmem_limit_bytes=8 * 2**20),
         cost_estimate=pl.CostEstimate(
-            flops=2000000000, bytes_accessed=2097152, transcendentals=0
+            flops=4 * 10**9, bytes_accessed=2**19, transcendentals=0
         ),
-        name="masks",
-    )(place, owners, alive_mask)
-    everyone, masks, scale = lax.optimization_barrier((everyone, masks, scale))
-    copies = pl.pallas_call(
-        pick_kernel,
-        out_shape=jax.ShapeDtypeStruct((GROUP, SOURCES * sta_count // GROUP, tiles.shape[3]), record.dtype),
-        in_specs=[in_smem(), in_vmem()],
-        out_specs=in_vmem(),
-        compiler_params=pltpu.CompilerParams(vmem_limit_bytes=8 * 2**20),
         name="pick_owners",
-    )(owners, everyone)
+    )(place, owners, everyone, alive_mask)
     groups = [list(range(first, first + GROUP)) for first in range(0, sta_count, GROUP)]
     gathered = lax.all_to_all(copies, "sta", 0, 0, axis_index_groups=groups)
 

time: 58.9 us -> 58.4 us (level)
  blocking collectives: 31.1 us -> 54.2 us
  waiting for transfers between devices: 10.6 us -> 0 us
  starting transfers between devices: 10.2 us -> 0 us
  local copies, waits for them, and re-layouts: 3.11 us -> 0.87 us
    all_to_all x0 -> x1, blocking collectives: none -> 23.1 us  [on_device(): everyone = lax.all_to_all(tiles, 'sta', 0, 0)]
    all_to_all x1 -> x0, waiting for transfers between devices: 10.6 us -> none  [on_device(): everyone = lax.all_to_all(tiles, 'sta', 0, 0)]
    all_to_all x1 -> x0, starting transfers between devices: 10.2 us -> none  [on_device(): everyone = lax.all_to_all(tiles, 'sta', 0, 0)]
    broadcast_in_dim x1 -> x0, local copies, waits for them, and re-layouts: 1.59 us -> none  [on_device(): jnp.broadcast_to(record[None], (sta_count // GROUP,) + record.shape)]
    unnamed x14, local copies, waits for them, and re-layouts: 1.52 us -> 0.87 us
  transfers between devices with their start and end apart: 1 -> 0, of which waited for: 1 -> 0; matrix products, arithmetic and copies ran while one was open for 0% -> 0% of each run, Pallas kernels for 1% -> 0%
where the time goes in v7:
time: 58.4 us; the launch traced here: 58.1 us
  blocking collectives  54.2 us (93%)
  Pallas kernels  2.94 us (5%)
  local copies, waits for them, and re-layouts  0.87 us (1%)
    all_to_all x1, blocking collectives, on_device(): everyone = lax.all_to_all(tiles, 'sta', 0, 0)  23.1 us
    all_to_all x1, blocking collectives, on_device(): parts = lax.all_to_all(pieces, 'day', 0, 0)  20.4 us
    all_to_all x1, blocking collectives, on_device(): gathered = lax.all_to_all(copies, 'sta', 0, 0, axis_index_groups=groups)  10.7 us
    pallas_call x1, Pallas kernels, on_device(): pl.pallas_call(cross_kernel, out_shape=jax.ShapeDtypeStruct((day_count, 2...  1.37 us

profile of v7, /device:TPU:8, one launch (start us, length us, event | category | flops | bytes accessed | tf_op | source)
XLA Modules:
  0.0 58.1 jit_solution(12315455402889551511)
XLA Ops:
  0.0 0.1 pad_add_fusion.place_ref
  0.1 0.0 copy-start.2
  0.1 0.8 %copy-done.2 = bf16[4,8,1024]{2,1,0:T(8,128)(2,1)S(1)} copy-done((bf16[4,8,1024]{2,1,0:T(8,128)(2,1)S(1)}, bf16[4,8,1024]{2,1,0:T(8,128)(2,1)}, u32[]{:S(2)}) %copy-start.2) | copy-done | bytes 65560
  0.9 0.0 copy-start.5
  0.9 0.0 copy-start.6
  0.9 23.1 %all_to_all.15.tiles_ref = bf16[32,4,8,128]{3,2,1,0:T(8,128)(2,1)S(1)} all-to-all(bf16[32,4,8,128]{3,2,1,0:T(8,128)(2,1)S(1)} %bitcast.10), channel_id=1, replica_groups=mesh['day'=16,'sta'=32] {'sta'}, dimensions={0} | all-to-all | bytes 524288 | tf_op jit(solution)/shard_map/all_to_all | solution.py:229
  24.0 0.0 copy-done.5
  24.0 0.0 copy-done.6
  24.0 0.0 copy-start
  24.0 0.0 copy-start.1
  24.1 0.0 copy-start.3
  24.1 0.0 copy-start.4
  24.1 0.8 %pick_owners.1 = (bf16[8,128,128]{2,1,0:T(8,128)(2,1)S(1)}, f32[160,128]{1,0:T(8,128)S(1)}, f32[32,128]{1,0:T(8,128)S(1)}) custom-call(s32[2]{0:T(128)S(1)} %pad_add_fusion.place_ref, s32[4]{0:T(128)S(1)} %copy-done.6, bf16[32,4,8,128]{3,2,1,0:T(8,128)(2,1)S(1)} %all_to_all.15.tiles_ref, s32[64,256]{1,0:T(8,128)S(1)} %copy-done.5), custom_call_target="tpu_custom_call" | custom-call | flops 4000000000 | bytes 524288 | tf_op jit(solution)/shard_map/pick_owners/pallas_call | solution.py:231
  24.9 10.7 %all_to_all.16 = bf16[8,128,128]{2,1,0:T(8,128)(2,1)S(1)} all-to-all(bf16[8,128,128]{2,1,0:T(8,128)(2,1)S(1)} %get-tuple-element.12), channel_id=1, replica_groups={{0,1,2,3,4,5,6,7},{8,9,10,11,12,13,14,15},{16,17,18,19,20,21,22,23},{24..., dimensions={0} | all-to-all | bytes 524288 | tf_op jit(solution)/shard_map/all_to_all | solution.py:249
  35.6 0.0 copy-done
  35.6 0.0 copy-done.1
  35.6 0.0 copy-done.3
  35.6 0.0 copy-done.4
  35.6 1.4 %cross_lags.1 = bf16[16,40,128]{2,1,0:T(8,128)(2,1)S(1)} custom-call(bf16[32,1024]{1,0:T(8,128)(2,1)S(1)} %bitcast.11, bf16[1024,128]{1,0:T(8,128)(2,1)S(1)} %bitcast.9, f32[160,128]{1,0:T(8,128)S(1)} %get-tuple-element.13.masks_ref, bf16[1024,1024]{1,0:T(8,128)(2,1)S(1)} %copy-done, bf16[1024,256]{1,0:T(8,128)(2,1)S(1)} %copy-done.1, ...), custom_call_target="tpu_custom_call" | custom-call | tf_op jit(solution)/shard_map/cross_lags/pallas_call | solution.py:251
  37.0 20.4 %all_to_all.17.parts_ref = bf16[16,40,128]{2,1,0:T(8,128)(2,1)S(1)} all-to-all(bf16[16,40,128]{2,1,0:T(8,128)(2,1)S(1)} %cross_lags.1), channel_id=1, replica_groups=mesh['day'=16,'sta'=32] {'day'}, dimensions={0} | all-to-all | bytes 327680 | tf_op jit(solution)/shard_map/all_to_all | solution.py:267
  57.4 0.7 %sum_parts.1 = f32[8,2,257]{2,1,0:T(2,128)} custom-call(bf16[16,40,128]{2,1,0:T(8,128)(2,1)S(1)} %all_to_all.17.parts_ref, f32[32,128]{1,0:T(8,128)S(1)} %get-tuple-element.14.scale_ref), custom_call_target="tpu_custom_call" | custom-call | tf_op jit(solution)/shard_map/sum_parts/pallas_call | solution.py:268
  (1 shorter events, 0.0 us)
Async XLA Ops:
  0.1 0.8 %copy-start.2 = (bf16[4,8,1024]{2,1,0:T(8,128)(2,1)S(1)}, bf16[4,8,1024]{2,1,0:T(8,128)(2,1)}, u32[]{:S(2)}) copy-start(bf16[4,8,1024]{2,1,0:T(8,128)(2,1)} %record_ref) | copy-start | bytes 196612
  0.9 23.1 %copy-start.5 = (s32[64,256]{1,0:T(8,128)S(1)}, s32[64,256]{1,0:T(8,128)}, u32[]{:S(2)}) copy-start(s32[64,256]{1,0:T(8,128)} %mask_ref.1) | copy-start | bytes 196612
  0.9 23.1 %copy-start.6 = (s32[4]{0:T(128)S(1)}, s32[4]{0:T(128)}, u32[]{:S(2)}) copy-start(s32[4]{0:T(128)} %owners_ref.1) | copy-start | bytes 52
  24.0 11.6 %copy-start = (bf16[1024,1024]{1,0:T(8,128)(2,1)S(1)}, bf16[1024,1024]{1,0:T(8,128)(2,1)}, u32[]{:S(2)}) copy-start(bf16[1024,1024]{1,0:T(8,128)(2,1)} %constant.15.clone.forward_ref) | copy-start | bytes 6291460
  24.0 11.6 %copy-start.1 = (bf16[1024,256]{1,0:T(8,128)(2,1)S(1)}, bf16[1024,256]{1,0:T(8,128)(2,1)}, u32[]{:S(2)}) copy-start(bf16[1024,256]{1,0:T(8,128)(2,1)} %constant.16.clone.lag_ref) | copy-start | bytes 1572868
  24.1 11.6 %copy-start.3 = (bf16[4,8,1024]{2,1,0:T(8,128)(2,1)S(1)}, bf16[4,8,1024]{2,1,0:T(8,128)(2,1)}, u32[]{:S(2)}) copy-start(bf16[4,8,1024]{2,1,0:T(8,128)(2,1)} %record_ref) | copy-start | bytes 196612
  24.1 11.6 %copy-start.4 = (bf16[16,1024]{1,0:T(8,128)(2,1)S(1)}, bf16[16,1024]{1,0:T(8,128)(2,1)}, u32[]{:S(2)}) copy-start(bf16[16,1024]{1,0:T(8,128)(2,1)} %constant.17.clone.last_ref) | copy-start | bytes 98308

commit v8 on v7

--- a/solution.py
+++ b/solution.py
@@ -13,6 +13,7 @@
 SHARE = 4
 SOURCES = 32
 GROUP = 8
+SLOTS = 3
 
 
 def forward_table(samples, half_len):
@@ -104,6 +105,21 @@
         out_ref[copy] = record_ref[...]
 
 
+def plane_of(sta):
+    return lax.rem(lax.div(sta, 2), 2)
+
+
+def slots_of(owners_ref):
+    planes = [plane_of(owners_ref[which]) for which in range(OWNERS)]
+    places = []
+    for which in range(OWNERS):
+        place = jnp.int32(0)
+        for other in range(which):
+            place = place + jnp.where(planes[other] == planes[which], 1, 0)
+        places.append(place)
+    return planes, places
+
+
 def pick_kernel(
     place_ref, owners_ref, tiles_ref, mask_ref, out_ref, masks_ref, scale_ref
 ):
@@ -111,35 +127,42 @@
         place_ref, owners_ref, mask_ref, scale_ref.shape[0] // 2, scale_ref.shape[1]
     )
     masks_ref[...] = jnp.broadcast_to(column, masks_ref.shape)
-    picked = jnp.concatenate(
-        [
-            tiles_ref[owners_ref[which], part]
-            for part in range(tiles_ref.shape[1])
-            for which in range(OWNERS)
-        ],
-        axis=0,
-    )
-    for copy in range(out_ref.shape[0]):
-        out_ref[copy] = picked
+    mine = plane_of(place_ref[1])
+    planes, places = slots_of(owners_ref)
+    parts = tiles_ref.shape[1]
+    for slot in range(SLOTS):
+        sender = jnp.int32(0)
+        for which in range(OWNERS):
+            owner = owners_ref[which]
+            chosen = jnp.logical_and(planes[which] == mine, places[which] == slot)
+            sender = jnp.where(chosen, lax.div(owner, 4) * 2 + lax.rem(owner, 2), sender)
+        for part in range(parts):
+            tile = tiles_ref[sender, part]
+            for copy in range(out_ref.shape[0]):
+                out_ref[copy, slot * parts + part] = tile
 
 
 def cross_kernel(
-    own_ref, tiles_ref, masks_ref, forward_ref, lag_ref, last_ref, out_ref, white_re, white_im
+    owners_ref, own_ref, tiles_ref, masks_ref, forward_ref, lag_ref, last_ref, out_ref, white_re, white_im
 ):
     width = own_ref.shape[0] // SHARE
     sources = masks_ref.shape[0] // SHARE - width
     half_len = white_re.shape[1]
-    tiles = tiles_ref.shape[0] // sources
-    wide = tiles // SHARE
+    planes, places = slots_of(owners_ref)
+    wide = tiles_ref.shape[0] // (GROUP * SLOTS)
     rows = []
     for w in range(SHARE):
+        device = w // 2 * 4 + w % 2
+        starts = [
+            ((device + 2 * plane) * SLOTS + place) * wide for plane, place in zip(planes, places)
+        ]
         rows.append(
             jnp.concatenate(
                 [
-                    tiles_ref[t * sources : (t + 1) * sources, :]
-                    for t in range(w * wide, (w + 1) * wide)
+                    jnp.concatenate([tiles_ref[start + k] for k in range(wide)], axis=1)
+                    for start in starts
                 ],
-                axis=1,
+                axis=0,
             )
         )
     rows.append(own_ref[...])
@@ -224,16 +247,19 @@
         ),
         name="spread",
     )(record)
-    tiles = blocks.reshape(sta_count // GROUP, w_dev, sta_dev, sta_count // w_dev, -1)
-    tiles = tiles.transpose(0, 1, 3, 2, 4).reshape(sta_count, sta_count // GROUP, sta_dev, -1)
-    everyone = lax.all_to_all(tiles, "sta", 0, 0)
+    wide = sta_count // w_dev
+    tiles = blocks.reshape(sta_count // GROUP, w_dev, sta_dev, wide, -1)
+    tiles = tiles.transpose(0, 1, 3, 2, 4).reshape(sta_count // 2, wide, sta_dev, -1)
+    planes = [
+        [4 * y + 2 * far + core for y in range(sta_count // 4) for core in range(2)]
+        for far in range(2)
+    ]
+    everyone = lax.all_to_all(tiles, "sta", 0, 0, axis_index_groups=planes)
 
     copies, masks, scale = pl.pallas_call(
         pick_kernel,
         out_shape=[
-            jax.ShapeDtypeStruct(
-                (GROUP, SOURCES * sta_count // GROUP, tiles.shape[3]), record.dtype
-            ),
+            jax.ShapeDtypeStruct((GROUP, SLOTS * wide) + tiles.shape[2:], record.dtype),
             jax.ShapeDtypeStruct((w_dev * (sources + sta_dev), 128), jnp.float32),
             jax.ShapeDtypeStruct((2 * rows, 128), jnp.float32),
         ],
@@ -251,14 +277,15 @@
     pieces = pl.pallas_call(
         cross_kernel,
         out_shape=jax.ShapeDtypeStruct((day_count, 2 * rows + 8, 128), jnp.bfloat16),
-        in_specs=[in_vmem()] * 6,
+        in_specs=[in_smem()] + [in_vmem()] * 6,
         out_specs=in_vmem(),
         scratch_shapes=[pltpu.VMEM((w_dev * (sources + sta_dev), half_len), jnp.float32)] * 2,
         compiler_params=pltpu.CompilerParams(vmem_limit_bytes=24 * 2**20),
         name="cross_lags",
     )(
+        owners,
         record.reshape(w_dev * sta_dev, samples),
-        gathered.reshape(sta_count * sources, -1),
+        gathered.reshape((-1,) + tiles.shape[2:]),
         masks,
         forward,
         lag_rows,

time: 58.4 us -> 57.1 us (0.978)
  blocking collectives: 54.2 us -> 52.3 us
    all_to_all x1, blocking collectives: 23.1 us -> 18.1 us  [on_device(): everyone = lax.all_to_all(tiles, 'sta', 0, 0, axis_index_groups=planes)]
    all_to_all x1, blocking collectives: 10.7 us -> 13.7 us  [on_device(): gathered = lax.all_to_all(copies, 'sta', 0, 0, axis_index_groups=groups)]
where the time goes in v8:
time: 57.1 us; the launch traced here: 56.8 us
  blocking collectives  52.3 us (92%)
  Pallas kernels  3.52 us (6%)
  local copies, waits for them, and re-layouts  0.87 us (2%)
    all_to_all x1, blocking collectives, on_device(): parts = lax.all_to_all(pieces, 'day', 0, 0)  20.5 us
    all_to_all x1, blocking collectives, on_device(): everyone = lax.all_to_all(tiles, 'sta', 0, 0, axis_index_groups=planes)  18.1 us
    all_to_all x1, blocking collectives, on_device(): gathered = lax.all_to_all(copies, 'sta', 0, 0, axis_index_groups=groups)  13.7 us
    pallas_call x1, Pallas kernels, on_device(): pl.pallas_call(cross_kernel, out_shape=jax.ShapeDtypeStruct((day_count, 2...  1.94 us

profile of v8, /device:TPU:8, one launch (start us, length us, event | category | flops | bytes accessed | tf_op | source)
XLA Modules:
  0.0 56.8 jit_solution(2356469195492834648)
XLA Ops:
  0.0 0.1 pad_add_fusion.place_ref
  0.1 0.0 copy-start.2
  0.1 0.8 %copy-done.2 = bf16[4,8,1024]{2,1,0:T(8,128)(2,1)S(1)} copy-done((bf16[4,8,1024]{2,1,0:T(8,128)(2,1)S(1)}, bf16[4,8,1024]{2,1,0:T(8,128)(2,1)}, u32[]{:S(2)}) %copy-start.2) | copy-done | bytes 65560
  0.9 0.0 copy-start.5
  0.9 0.0 copy-start.6
  0.9 18.1 %all_to_all.15.tiles_ref = bf16[16,8,8,128]{3,2,1,0:T(8,128)(2,1)S(1)} all-to-all(bf16[16,8,8,128]{3,2,1,0:T(8,128)(2,1)S(1)} %bitcast.10), channel_id=1, replica_groups={{0,1,4,5,8,9,12,13,16,17,20,21,24,25,28,29},{2,3,6,7,10,11,14,15,18,19,..., dimensions={0} | all-to-all | bytes 524288 | tf_op jit(solution)/shard_map/all_to_all | solution.py:257
  19.0 0.0 copy-done.5
  19.0 0.0 copy-done.6
  19.0 0.0 copy-start
  19.0 0.0 copy-start.1
  19.0 0.0 copy-start.3
  19.1 0.0 copy-start.4
  19.1 0.9 %pick_owners.1 = (bf16[8,24,8,128]{3,2,1,0:T(8,128)(2,1)S(1)}, f32[160,128]{1,0:T(8,128)S(1)}, f32[32,128]{1,0:T(8,128)S(1)}) custom-call(s32[2]{0:T(128)S(1)} %pad_add_fusion.place_ref, s32[4]{0:T(128)S(1)} %copy-done.5, bf16[16,8,8,128]{3,2,1,0:T(8,128)(2,1)S(1)} %all_to_all.15.tiles_ref, s32[64,256]{1,0:T(8,128)S(1)} %copy-done.6), custom_call_target="tpu_custom_call" | custom-call | flops 4000000000 | bytes 524288 | tf_op jit(solution)/shard_map/pick_owners/pallas_call | solution.py:259
  19.9 13.7 %all_to_all.16 = bf16[8,24,8,128]{3,2,1,0:T(8,128)(2,1)S(1)} all-to-all(bf16[8,24,8,128]{3,2,1,0:T(8,128)(2,1)S(1)} %get-tuple-element.12), channel_id=1, replica_groups={{0,1,2,3,4,5,6,7},{8,9,10,11,12,13,14,15},{16,17,18,19,20,21,22,23},{24..., dimensions={0} | all-to-all | bytes 786432 | tf_op jit(solution)/shard_map/all_to_all | solution.py:275
  33.6 0.0 copy-done
  33.6 0.0 copy-done.1
  33.6 0.0 copy-done.3
  33.6 0.0 copy-done.4
  33.7 1.9 %cross_lags.1 = bf16[16,40,128]{2,1,0:T(8,128)(2,1)S(1)} custom-call(s32[4]{0:T(128)S(1)} %copy-done.5, bf16[32,1024]{1,0:T(8,128)(2,1)S(1)} %bitcast.11, bf16[192,8,128]{2,1,0:T(8,128)(2,1)S(1)} %bitcast.9, f32[160,128]{1,0:T(8,128)S(1)} %get-tuple-element.13.masks_ref, bf16[1024,1024]{1,0:T(8,128)(2,1)S(1)} %copy-done, bf16[1024,256]{1,0:T(8,128)(2,1)S(1)} %copy-done.1, ...), custom_call_target="tpu_custom_call" | custom-call | tf_op jit(solution)/shard_map/cross_lags/pallas_call | solution.py:277
  35.6 20.5 %all_to_all.17.parts_ref = bf16[16,40,128]{2,1,0:T(8,128)(2,1)S(1)} all-to-all(bf16[16,40,128]{2,1,0:T(8,128)(2,1)S(1)} %cross_lags.1), channel_id=1, replica_groups=mesh['day'=16,'sta'=32] {'day'}, dimensions={0} | all-to-all | bytes 327680 | tf_op jit(solution)/shard_map/all_to_all | solution.py:294
  56.1 0.7 %sum_parts.1 = f32[8,2,257]{2,1,0:T(2,128)} custom-call(bf16[16,40,128]{2,1,0:T(8,128)(2,1)S(1)} %all_to_all.17.parts_ref, f32[32,128]{1,0:T(8,128)S(1)} %get-tuple-element.14.scale_ref), custom_call_target="tpu_custom_call" | custom-call | tf_op jit(solution)/shard_map/sum_parts/pallas_call | solution.py:295
  (1 shorter events, 0.0 us)
Async XLA Ops:
  0.1 0.8 %copy-start.2 = (bf16[4,8,1024]{2,1,0:T(8,128)(2,1)S(1)}, bf16[4,8,1024]{2,1,0:T(8,128)(2,1)}, u32[]{:S(2)}) copy-start(bf16[4,8,1024]{2,1,0:T(8,128)(2,1)} %record_ref) | copy-start | bytes 196612
  0.9 18.1 %copy-start.5 = (s32[4]{0:T(128)S(1)}, s32[4]{0:T(128)}, u32[]{:S(2)}) copy-start(s32[4]{0:T(128)} %owners_ref.3) | copy-start | bytes 52
  0.9 18.1 %copy-start.6 = (s32[64,256]{1,0:T(8,128)S(1)}, s32[64,256]{1,0:T(8,128)}, u32[]{:S(2)}) copy-start(s32[64,256]{1,0:T(8,128)} %mask_ref.1) | copy-start | bytes 196612
  19.0 14.6 %copy-start = (bf16[1024,1024]{1,0:T(8,128)(2,1)S(1)}, bf16[1024,1024]{1,0:T(8,128)(2,1)}, u32[]{:S(2)}) copy-start(bf16[1024,1024]{1,0:T(8,128)(2,1)} %constant.15.clone.forward_ref) | copy-start | bytes 6291460
  19.0 14.6 %copy-start.1 = (bf16[1024,256]{1,0:T(8,128)(2,1)S(1)}, bf16[1024,256]{1,0:T(8,128)(2,1)}, u32[]{:S(2)}) copy-start(bf16[1024,256]{1,0:T(8,128)(2,1)} %constant.16.clone.lag_ref) | copy-start | bytes 1572868
  19.0 14.6 %copy-start.3 = (bf16[4,8,1024]{2,1,0:T(8,128)(2,1)S(1)}, bf16[4,8,1024]{2,1,0:T(8,128)(2,1)}, u32[]{:S(2)}) copy-start(bf16[4,8,1024]{2,1,0:T(8,128)(2,1)} %record_ref) | copy-start | bytes 196612
  19.1 14.6 %copy-start.4 = (bf16[16,1024]{1,0:T(8,128)(2,1)S(1)}, bf16[16,1024]{1,0:T(8,128)(2,1)}, u32[]{:S(2)}) copy-start(bf16[16,1024]{1,0:T(8,128)(2,1)} %constant.17.clone.last_ref) | copy-start | bytes 98308

commit v9 on v8

--- a/solution.py
+++ b/solution.py
@@ -126,9 +126,17 @@
     column, scale_ref[...] = mask_columns(
         place_ref, owners_ref, mask_ref, scale_ref.shape[0] // 2, scale_ref.shape[1]
     )
-    masks_ref[...] = jnp.broadcast_to(column, masks_ref.shape)
+    lanes = masks_ref.shape[1]
+    row = lax.broadcasted_iota(jnp.int32, (OWNERS * 2 * SLOTS, lanes), 0)
+    planes, places = slots_of(owners_ref)
+    held = jnp.zeros(row.shape, jnp.float32)
+    for which in range(OWNERS):
+        at = (2 * which + planes[which]) * SLOTS + places[which]
+        held = held + jnp.where(row == at, 1.0, 0.0)
+    masks_ref[...] = jnp.concatenate(
+        [jnp.broadcast_to(column, (column.shape[0], lanes)), held], axis=0
+    )
     mine = plane_of(place_ref[1])
-    planes, places = slots_of(owners_ref)
     parts = tiles_ref.shape[1]
     for slot in range(SLOTS):
         sender = jnp.int32(0)
@@ -143,31 +151,45 @@
 
 
 def cross_kernel(
-    owners_ref, own_ref, tiles_ref, masks_ref, forward_ref, lag_ref, last_ref, out_ref, white_re, white_im
+    own_ref, tiles_ref, masks_ref, forward_ref, lag_ref, last_ref, out_ref, white_re, white_im
 ):
     width = own_ref.shape[0] // SHARE
-    sources = masks_ref.shape[0] // SHARE - width
+    sources = SOURCES
+    marks = SHARE * (sources + width)
     half_len = white_re.shape[1]
-    planes, places = slots_of(owners_ref)
     wide = tiles_ref.shape[0] // (GROUP * SLOTS)
+    slots = 2 * SLOTS
+    held = [
+        [
+            jnp.broadcast_to(masks_ref[pl.ds(marks + which * slots + n, 1), :], (width, 128)) > 0
+            for n in range(slots)
+        ]
+        for which in range(OWNERS)
+    ]
     rows = []
     for w in range(SHARE):
         device = w // 2 * 4 + w % 2
-        starts = [
-            ((device + 2 * plane) * SLOTS + place) * wide for plane, place in zip(planes, places)
-        ]
+        blocks = [[] for _ in range(OWNERS)]
+        for k in range(wide):
+            tiles = [
+                tiles_ref[((device + 2 * (n // SLOTS)) * SLOTS + n % SLOTS) * wide + k].astype(
+                    jnp.float32
+                )
+                for n in range(slots)
+            ]
+            for which in range(OWNERS):
+                tile = tiles[0]
+                for n in range(1, slots):
+                    tile = jnp.where(held[which][n], tiles[n], tile)
+                blocks[which].append(tile)
         rows.append(
-            jnp.concatenate(
-                [
-                    jnp.concatenate([tiles_ref[start + k] for k in range(wide)], axis=1)
-                    for start in starts
-                ],
-                axis=0,
+            jnp.concatenate([jnp.concatenate(b, axis=1) for b in blocks], axis=0).astype(
+                own_ref.dtype
             )
         )
     rows.append(own_ref[...])
     white_re[...], white_im[...] = whiten(
-        jnp.concatenate(rows, axis=0), forward_ref, masks_ref[:, 0:1]
+        jnp.concatenate(rows, axis=0), forward_ref, masks_ref[0:marks, 0:1]
     )
     first_own = SHARE * sources
     crossed = []
@@ -260,7 +282,9 @@
         pick_kernel,
         out_shape=[
             jax.ShapeDtypeStruct((GROUP, SLOTS * wide) + tiles.shape[2:], record.dtype),
-            jax.ShapeDtypeStruct((w_dev * (sources + sta_dev), 128), jnp.float32),
+            jax.ShapeDtypeStruct(
+                (w_dev * (sources + sta_dev) + OWNERS * 2 * SLOTS, 128), jnp.float32
+            ),
             jax.ShapeDtypeStruct((2 * rows, 128), jnp.float32),
         ],
         in_specs=[in_smem(), in_smem()] + [in_vmem()] * 2,
@@ -277,13 +301,12 @@
     pieces = pl.pallas_call(
         cross_kernel,
         out_shape=jax.ShapeDtypeStruct((day_count, 2 * rows + 8, 128), jnp.bfloat16),
-        in_specs=[in_smem()] + [in_vmem()] * 6,
+        in_specs=[in_vmem()] * 6,
         out_specs=in_vmem(),
         scratch_shapes=[pltpu.VMEM((w_dev * (sources + sta_dev), half_len), jnp.float32)] * 2,
         compiler_params=pltpu.CompilerParams(vmem_limit_bytes=24 * 2**20),
         name="cross_lags",
     )(
-        owners,
         record.reshape(w_dev * sta_dev, samples),
         gathered.reshape((-1,) + tiles.shape[2:]),
         masks,

time: 57.1 us -> 56.5 us (0.989)
  no operation moved by 1% of the time
where the time goes in v9:
time: 56.5 us; the launch traced here: 56.2 us
  blocking collectives  52.2 us (92%)
  Pallas kernels  2.98 us (5%)
  local copies, waits for them, and re-layouts  0.87 us (2%)
    all_to_all x1, blocking collectives, on_device(): parts = lax.all_to_all(pieces, 'day', 0, 0)  20.5 us
    all_to_all x1, blocking collectives, on_device(): everyone = lax.all_to_all(tiles, 'sta', 0, 0, axis_index_groups=planes)  18.1 us
    all_to_all x1, blocking collectives, on_device(): gathered = lax.all_to_all(copies, 'sta', 0, 0, axis_index_groups=groups)  13.7 us
    pallas_call x1, Pallas kernels, on_device(): pl.pallas_call(cross_kernel, out_shape=jax.ShapeDtypeStruct((day_count, 2...  1.42 us

profile of v9, /device:TPU:8, one launch (start us, length us, event | category | flops | bytes accessed | tf_op | source)
XLA Modules:
  0.0 56.2 jit_solution(5411368229975350332)
XLA Ops:
  0.0 0.1 pad_add_fusion.place_ref
  0.1 0.0 copy-start.2
  0.1 0.8 %copy-done.2 = bf16[4,8,1024]{2,1,0:T(8,128)(2,1)S(1)} copy-done((bf16[4,8,1024]{2,1,0:T(8,128)(2,1)S(1)}, bf16[4,8,1024]{2,1,0:T(8,128)(2,1)}, u32[]{:S(2)}) %copy-start.2) | copy-done | bytes 65560
  0.9 0.0 copy-start.5
  0.9 0.0 copy-start.6
  0.9 18.1 %all_to_all.15.tiles_ref = bf16[16,8,8,128]{3,2,1,0:T(8,128)(2,1)S(1)} all-to-all(bf16[16,8,8,128]{3,2,1,0:T(8,128)(2,1)S(1)} %bitcast.10), channel_id=1, replica_groups={{0,1,4,5,8,9,12,13,16,17,20,21,24,25,28,29},{2,3,6,7,10,11,14,15,18,19,..., dimensions={0} | all-to-all | bytes 524288 | tf_op jit(solution)/shard_map/all_to_all | solution.py:279
  19.0 0.0 copy-done.5
  19.0 0.0 copy-done.6
  19.0 0.0 copy-start
  19.0 0.0 copy-start.1
  19.0 0.0 copy-start.3
  19.1 0.0 copy-start.4
  19.1 0.8 %pick_owners.1 = (bf16[8,24,8,128]{3,2,1,0:T(8,128)(2,1)S(1)}, f32[184,128]{1,0:T(8,128)S(1)}, f32[32,128]{1,0:T(8,128)S(1)}) custom-call(s32[2]{0:T(128)S(1)} %pad_add_fusion.place_ref, s32[4]{0:T(128)S(1)} %copy-done.6, bf16[16,8,8,128]{3,2,1,0:T(8,128)(2,1)S(1)} %all_to_all.15.tiles_ref, s32[64,256]{1,0:T(8,128)S(1)} %copy-done.5), custom_call_target="tpu_custom_call" | custom-call | flops 4000000000 | bytes 524288 | tf_op jit(solution)/shard_map/pick_owners/pallas_call | solution.py:281
  19.9 13.7 %all_to_all.16 = bf16[8,24,8,128]{3,2,1,0:T(8,128)(2,1)S(1)} all-to-all(bf16[8,24,8,128]{3,2,1,0:T(8,128)(2,1)S(1)} %get-tuple-element.12), channel_id=1, replica_groups={{0,1,2,3,4,5,6,7},{8,9,10,11,12,13,14,15},{16,17,18,19,20,21,22,23},{24..., dimensions={0} | all-to-all | bytes 786432 | tf_op jit(solution)/shard_map/all_to_all | solution.py:299
  33.6 0.0 copy-done
  33.6 0.0 copy-done.1
  33.6 0.0 copy-done.3
  33.6 0.0 copy-done.4
  33.6 1.4 %cross_lags.1 = bf16[16,40,128]{2,1,0:T(8,128)(2,1)S(1)} custom-call(bf16[32,1024]{1,0:T(8,128)(2,1)S(1)} %bitcast.11, bf16[192,8,128]{2,1,0:T(8,128)(2,1)S(1)} %bitcast.9, f32[184,128]{1,0:T(8,128)S(1)} %get-tuple-element.13.masks_ref, bf16[1024,1024]{1,0:T(8,128)(2,1)S(1)} %copy-done, bf16[1024,256]{1,0:T(8,128)(2,1)S(1)} %copy-done.1, ...), custom_call_target="tpu_custom_call" | custom-call | tf_op jit(solution)/shard_map/cross_lags/pallas_call | solution.py:301
  35.1 20.5 %all_to_all.17.parts_ref = bf16[16,40,128]{2,1,0:T(8,128)(2,1)S(1)} all-to-all(bf16[16,40,128]{2,1,0:T(8,128)(2,1)S(1)} %cross_lags.1), channel_id=1, replica_groups=mesh['day'=16,'sta'=32] {'day'}, dimensions={0} | all-to-all | bytes 327680 | tf_op jit(solution)/shard_map/all_to_all | solution.py:317
  55.5 0.7 %sum_parts.1 = f32[8,2,257]{2,1,0:T(2,128)} custom-call(bf16[16,40,128]{2,1,0:T(8,128)(2,1)S(1)} %all_to_all.17.parts_ref, f32[32,128]{1,0:T(8,128)S(1)} %get-tuple-element.14.scale_ref), custom_call_target="tpu_custom_call" | custom-call | tf_op jit(solution)/shard_map/sum_parts/pallas_call | solution.py:318
  (1 shorter events, 0.0 us)
Async XLA Ops:
  0.1 0.8 %copy-start.2 = (bf16[4,8,1024]{2,1,0:T(8,128)(2,1)S(1)}, bf16[4,8,1024]{2,1,0:T(8,128)(2,1)}, u32[]{:S(2)}) copy-start(bf16[4,8,1024]{2,1,0:T(8,128)(2,1)} %record_ref) | copy-start | bytes 196612
  0.9 18.1 %copy-start.5 = (s32[64,256]{1,0:T(8,128)S(1)}, s32[64,256]{1,0:T(8,128)}, u32[]{:S(2)}) copy-start(s32[64,256]{1,0:T(8,128)} %mask_ref.1) | copy-start | bytes 196612
  0.9 18.1 %copy-start.6 = (s32[4]{0:T(128)S(1)}, s32[4]{0:T(128)}, u32[]{:S(2)}) copy-start(s32[4]{0:T(128)} %owners_ref.1) | copy-start | bytes 52
  19.0 14.6 %copy-start = (bf16[1024,1024]{1,0:T(8,128)(2,1)S(1)}, bf16[1024,1024]{1,0:T(8,128)(2,1)}, u32[]{:S(2)}) copy-start(bf16[1024,1024]{1,0:T(8,128)(2,1)} %constant.15.clone.forward_ref) | copy-start | bytes 6291460
  19.0 14.6 %copy-start.1 = (bf16[1024,256]{1,0:T(8,128)(2,1)S(1)}, bf16[1024,256]{1,0:T(8,128)(2,1)}, u32[]{:S(2)}) copy-start(bf16[1024,256]{1,0:T(8,128)(2,1)} %constant.16.clone.lag_ref) | copy-start | bytes 1572868
  19.0 14.6 %copy-start.3 = (bf16[4,8,1024]{2,1,0:T(8,128)(2,1)S(1)}, bf16[4,8,1024]{2,1,0:T(8,128)(2,1)}, u32[]{:S(2)}) copy-start(bf16[4,8,1024]{2,1,0:T(8,128)(2,1)} %record_ref) | copy-start | bytes 196612
  19.1 14.6 %copy-start.4 = (bf16[16,1024]{1,0:T(8,128)(2,1)S(1)}, bf16[16,1024]{1,0:T(8,128)(2,1)}, u32[]{:S(2)}) copy-start(bf16[16,1024]{1,0:T(8,128)(2,1)} %constant.17.clone.last_ref) | copy-start | bytes 98308

commit v10 on v9

--- a/solution.py
+++ b/solution.py
@@ -64,8 +64,7 @@
     )
 
 
-def mask_columns(place_ref, owners_ref, mask_ref, rows, lanes):
-    day_pos, sta_pos = place_ref[0], place_ref[1]
+def mask_columns(day_pos, sta_pos, owners_ref, mask_ref, rows, lanes):
     stations = mask_ref.shape[1]
     sources = SOURCES
     width = sources // OWNERS
@@ -121,10 +120,11 @@
 
 
 def pick_kernel(
-    place_ref, owners_ref, tiles_ref, mask_ref, out_ref, masks_ref, scale_ref
+    owners_ref, tiles_ref, mask_ref, out_ref, masks_ref, scale_ref
 ):
+    day_pos, sta_pos = lax.axis_index("day"), lax.axis_index("sta")
     column, scale_ref[...] = mask_columns(
-        place_ref, owners_ref, mask_ref, scale_ref.shape[0] // 2, scale_ref.shape[1]
+        day_pos, sta_pos, owners_ref, mask_ref, scale_ref.shape[0] // 2, scale_ref.shape[1]
     )
     lanes = masks_ref.shape[1]
     row = lax.broadcasted_iota(jnp.int32, (OWNERS * 2 * SLOTS, lanes), 0)
@@ -136,7 +136,7 @@
     masks_ref[...] = jnp.concatenate(
         [jnp.broadcast_to(column, (column.shape[0], lanes)), held], axis=0
     )
-    mine = plane_of(place_ref[1])
+    mine = plane_of(sta_pos)
     parts = tiles_ref.shape[1]
     for slot in range(SLOTS):
         sender = jnp.int32(0)
@@ -252,12 +252,9 @@
     forward = jnp.asarray(forward_table(samples, half_len))
     lag_rows, last_row = map(jnp.asarray, lag_table(samples, half_len, MAXLAG))
     day_count, sta_count = lax.axis_size("day"), lax.axis_size("sta")
-    day_pos, sta_pos = lax.axis_index("day"), lax.axis_index("sta")
     src_dev = sources // day_count
     rows = src_dev * sta_dev
-    place = jnp.stack([day_pos, sta_pos]).astype(jnp.int32)
-
-    record, place = lax.optimization_barrier((record, place))
+
     blocks = pl.pallas_call(
         spread_kernel,
         out_shape=jax.ShapeDtypeStruct((sta_count // GROUP,) + record.shape, record.dtype),
@@ -287,14 +284,14 @@
             ),
             jax.ShapeDtypeStruct((2 * rows, 128), jnp.float32),
         ],
-        in_specs=[in_smem(), in_smem()] + [in_vmem()] * 2,
+        in_specs=[in_smem()] + [in_vmem()] * 2,
         out_specs=[in_vmem()] * 3,
         compiler_params=pltpu.CompilerParams(vmem_limit_bytes=8 * 2**20),
         cost_estimate=pl.CostEstimate(
             flops=4 * 10**9, bytes_accessed=2**19, transcendentals=0
         ),
         name="pick_owners",
-    )(place, owners, everyone, alive_mask)
+    )(owners, everyone, alive_mask)
     groups = [list(range(first, first + GROUP)) for first in range(0, sta_count, GROUP)]
     gathered = lax.all_to_all(copies, "sta", 0, 0, axis_index_groups=groups)
 

time: 56.5 us -> 56.4 us (level)
  no operation moved by 1% of the time
where the time goes in v10:
time: 56.4 us; the launch traced here: 56.2 us
  blocking collectives  52.3 us (93%)
  Pallas kernels  2.98 us (5%)
  local copies, waits for them, and re-layouts  0.87 us (2%)
    all_to_all x1, blocking collectives, on_device(): parts = lax.all_to_all(pieces, 'day', 0, 0)  20.5 us
    all_to_all x1, blocking collectives, on_device(): everyone = lax.all_to_all(tiles, 'sta', 0, 0, axis_index_groups=planes)  18.1 us
    all_to_all x1, blocking collectives, on_device(): gathered = lax.all_to_all(copies, 'sta', 0, 0, axis_index_groups=groups)  13.7 us
    pallas_call x1, Pallas kernels, on_device(): pl.pallas_call(cross_kernel, out_shape=jax.ShapeDtypeStruct((day_count, 2...  1.42 us

profile of v10, /device:TPU:8, one launch (start us, length us, event | category | flops | bytes accessed | tf_op | source)
XLA Modules:
  0.0 56.2 jit_solution(9690565428601548184)
XLA Ops:
  0.0 0.0 copy-start.2
  0.0 0.8 %copy-done.2 = bf16[4,8,1024]{2,1,0:T(8,128)(2,1)S(1)} copy-done((bf16[4,8,1024]{2,1,0:T(8,128)(2,1)S(1)}, bf16[4,8,1024]{2,1,0:T(8,128)(2,1)}, u32[]{:S(2)}) %copy-start.2) | copy-done | bytes 65560
  0.8 0.0 copy-start.5
  0.8 0.0 copy-start.6
  0.9 18.1 %all_to_all.15.tiles_ref = bf16[16,8,8,128]{3,2,1,0:T(8,128)(2,1)S(1)} all-to-all(bf16[16,8,8,128]{3,2,1,0:T(8,128)(2,1)S(1)} %bitcast.8), channel_id=1, replica_groups={{0,1,4,5,8,9,12,13,16,17,20,21,24,25,28,29},{2,3,6,7,10,11,14,15,18,19,..., dimensions={0} | all-to-all | bytes 524288 | tf_op jit(solution)/shard_map/all_to_all | solution.py:276
  19.0 0.0 copy-done.5
  19.0 0.0 copy-done.6
  19.0 0.0 copy-start
  19.0 0.0 copy-start.1
  19.0 0.0 copy-start.3
  19.0 0.0 copy-start.4
  19.0 0.8 %pick_owners.1 = (bf16[8,24,8,128]{3,2,1,0:T(8,128)(2,1)S(1)}, f32[184,128]{1,0:T(8,128)S(1)}, f32[32,128]{1,0:T(8,128)S(1)}) custom-call(s32[4]{0:T(128)S(1)} %copy-done.6, bf16[16,8,8,128]{3,2,1,0:T(8,128)(2,1)S(1)} %all_to_all.15.tiles_ref, s32[64,256]{1,0:T(8,128)S(1)} %copy-done.5), custom_call_target="tpu_custom_call" | custom-call | flops 4000000000 | bytes 524288 | tf_op jit(solution)/shard_map/pick_owners/pallas_call | solution.py:278
  19.8 13.7 %all_to_all.16 = bf16[8,24,8,128]{3,2,1,0:T(8,128)(2,1)S(1)} all-to-all(bf16[8,24,8,128]{3,2,1,0:T(8,128)(2,1)S(1)} %get-tuple-element.8), channel_id=1, replica_groups={{0,1,2,3,4,5,6,7},{8,9,10,11,12,13,14,15},{16,17,18,19,20,21,22,23},{24..., dimensions={0} | all-to-all | bytes 786432 | tf_op jit(solution)/shard_map/all_to_all | solution.py:296
  33.5 0.0 copy-done
  33.5 0.0 copy-done.1
  33.5 0.0 copy-done.3
  33.5 0.0 copy-done.4
  33.6 1.4 %cross_lags.1 = bf16[16,40,128]{2,1,0:T(8,128)(2,1)S(1)} custom-call(bf16[32,1024]{1,0:T(8,128)(2,1)S(1)} %bitcast.9, bf16[192,8,128]{2,1,0:T(8,128)(2,1)S(1)} %bitcast.7, f32[184,128]{1,0:T(8,128)S(1)} %get-tuple-element.9.masks_ref, bf16[1024,1024]{1,0:T(8,128)(2,1)S(1)} %copy-done, bf16[1024,256]{1,0:T(8,128)(2,1)S(1)} %copy-done.1, ...), custom_call_target="tpu_custom_call" | custom-call | tf_op jit(solution)/shard_map/cross_lags/pallas_call | solution.py:298
  35.0 20.5 %all_to_all.17.parts_ref = bf16[16,40,128]{2,1,0:T(8,128)(2,1)S(1)} all-to-all(bf16[16,40,128]{2,1,0:T(8,128)(2,1)S(1)} %cross_lags.1), channel_id=1, replica_groups=mesh['day'=16,'sta'=32] {'day'}, dimensions={0} | all-to-all | bytes 327680 | tf_op jit(solution)/shard_map/all_to_all | solution.py:314
  55.5 0.7 %sum_parts.1 = f32[8,2,257]{2,1,0:T(2,128)} custom-call(bf16[16,40,128]{2,1,0:T(8,128)(2,1)S(1)} %all_to_all.17.parts_ref, f32[32,128]{1,0:T(8,128)S(1)} %get-tuple-element.10.scale_ref), custom_call_target="tpu_custom_call" | custom-call | tf_op jit(solution)/shard_map/sum_parts/pallas_call | solution.py:315
  (1 shorter events, 0.0 us)
Async XLA Ops:
  0.0 0.8 %copy-start.2 = (bf16[4,8,1024]{2,1,0:T(8,128)(2,1)S(1)}, bf16[4,8,1024]{2,1,0:T(8,128)(2,1)}, u32[]{:S(2)}) copy-start(bf16[4,8,1024]{2,1,0:T(8,128)(2,1)} %record_ref.1) | copy-start | bytes 196612
  0.8 18.1 %copy-start.5 = (s32[64,256]{1,0:T(8,128)S(1)}, s32[64,256]{1,0:T(8,128)}, u32[]{:S(2)}) copy-start(s32[64,256]{1,0:T(8,128)} %mask_ref.1) | copy-start | bytes 196612
  0.8 18.1 %copy-start.6 = (s32[4]{0:T(128)S(1)}, s32[4]{0:T(128)}, u32[]{:S(2)}) copy-start(s32[4]{0:T(128)} %owners_ref.1) | copy-start | bytes 52
  19.0 14.6 %copy-start = (bf16[1024,1024]{1,0:T(8,128)(2,1)S(1)}, bf16[1024,1024]{1,0:T(8,128)(2,1)}, u32[]{:S(2)}) copy-start(bf16[1024,1024]{1,0:T(8,128)(2,1)} %constant.6.clone.forward_ref) | copy-start | bytes 6291460
  19.0 14.6 %copy-start.1 = (bf16[1024,256]{1,0:T(8,128)(2,1)S(1)}, bf16[1024,256]{1,0:T(8,128)(2,1)}, u32[]{:S(2)}) copy-start(bf16[1024,256]{1,0:T(8,128)(2,1)} %constant.7.clone.lag_ref) | copy-start | bytes 1572868
  19.0 14.6 %copy-start.3 = (bf16[4,8,1024]{2,1,0:T(8,128)(2,1)S(1)}, bf16[4,8,1024]{2,1,0:T(8,128)(2,1)}, u32[]{:S(2)}) copy-start(bf16[4,8,1024]{2,1,0:T(8,128)(2,1)} %record_ref.1) | copy-start | bytes 196612
  19.0 14.6 %copy-start.4 = (bf16[16,1024]{1,0:T(8,128)(2,1)S(1)}, bf16[16,1024]{1,0:T(8,128)(2,1)}, u32[]{:S(2)}) copy-start(bf16[16,1024]{1,0:T(8,128)(2,1)} %constant.8.clone.last_ref) | copy-start | bytes 98308
